TPU v7x, 32 devices: a whole 2x2x4 slice. The times are simulated.
32 devices in a mesh: groups: 2 (over y), tm: 4 (over z), lat: 2 (over x), lon: 2 (over core).
Axes of the slice: x: 2, y: 2, z: 4, core: 2. Of those that a mesh axis runs over, the one named last changes fastest.
Arguments:
- prior_state: float32 [16, 8, 16, 256], P(('groups', 'tm'), None, 'lat', 'lon'), parts along dimension 0, may hold values from -6 to 6
- observed: float32 [16, 8, 16, 256], P(('groups', 'tm'), None, 'lat', 'lon'), parts along dimension 0, may hold values from -6 to 6
- obs_weight: float32 [16, 8, 16, 256], P(('groups', 'tm'), None, 'lat', 'lon'), parts along dimension 0, may hold values from 0 to 2
- noise_field: float32 [2, 16, 8, 16, 256], P(None, ('groups', 'tm'), None, 'lat', 'lon'), parts along dimension 1, may hold values from -6 to 6
- step_sizes: float32 [2], replicated, may hold values from 0.05 to 0.3
- lift_weight: float32 [96, 40], replicated, may hold values from -1 to 1
- conv_weights: bfloat16 [2, 9, 96, 96], replicated, may hold values from -0.21875 to 0.21875
- out_weight: bfloat16 [8, 96], replicated, may hold values from -0.625 to 0.625
Outputs:
- analysis: float32 [16, 8, 16, 256], P(('groups', 'tm'), None, 'lat', 'lon'), parts along dimension 0
There are 2 independent parts, one for each index of `groups`. A program takes and returns all parts, laid end to end along the dimension named above; an argument that names none is the same for every part. Nothing has to cross between parts.
All inputs are finite; a program needn't handle non-finite values.
Results may differ from a plain program's by a relative error of at most 0.0012.
Values may be sent and summed in bfloat16 or wider, within the bound.
A program may use at most 64 MiB of HBM per device.

v0:
```python
import jax
import jax.numpy as jnp
from jax import lax
from jax.sharding import PartitionSpec as P


def extended_2(block, sides, width, periodic):
    for axis, dim in sides:
        count = lax.axis_size(axis)
        forward = [(i, i + 1) for i in range(count - 1)]
        if periodic:
            forward.append((count - 1, 0))
        backward = [(target, source) for source, target in forward]
        low = lax.ppermute(
            lax.slice_in_dim(block, block.shape[dim] - width, None, axis=dim), axis, forward
        )
        high = lax.ppermute(lax.slice_in_dim(block, 0, width, axis=dim), axis, backward)
        block = jnp.concatenate([low, block, high], axis=dim)
    return block


def rim_rows(values, margin):
    row_count = values.shape[2]
    own_rows = row_count - 2 * margin
    row_start = lax.axis_index("lat") * own_rows - margin
    row_index = row_start + lax.iota(jnp.int32, row_count)
    inside = (row_index >= 0) & (row_index < own_rows * lax.axis_size("lat"))
    return values * inside.astype(values.dtype)[None, None, :, None]


def conv_valid(values, kernel):
    row_count = values.shape[2] - 2
    col_count = values.shape[3] - 2
    summed = jnp.zeros((values.shape[0], kernel.shape[1], row_count, col_count), jnp.float32)
    for row_off in range(3):
        for col_off in range(3):
            part = values[:, :, row_off : row_off + row_count, col_off : col_off + col_count]
            summed = summed + jnp.einsum(
                "oi,firw->forw",
                kernel[3 * row_off + col_off],
                part,
                preferred_element_type=jnp.float32,
            )
    return summed


def wide_border(values):
    return rim_rows(extended_2(values, (("lat", 2), ("lon", 3)), 2, True), 2)


def score_all(current, lift_weight, conv_weights, out_weight):
    frame_count = current.shape[0]
    extended = extended_2(current, (("tm", 0),), 2, False)
    stacked = jnp.concatenate(
        [extended[offset : offset + frame_count] for offset in range(5)], axis=1
    )
    lifted = jnp.einsum(
        "oc,fcrw->forw", lift_weight, stacked, precision=lax.Precision.HIGHEST
    ).astype(jnp.bfloat16)
    activated = jax.nn.silu(conv_valid(wide_border(lifted), conv_weights[0])).astype(jnp.bfloat16)
    activated = rim_rows(activated, 1)
    second = jax.nn.silu(conv_valid(activated, conv_weights[1]))
    merged = (lifted.astype(jnp.float32) + second).astype(jnp.bfloat16)
    return jnp.einsum("co,forw->fcrw", out_weight, merged, preferred_element_type=jnp.float32)


def per_device(
    prior_state,
    observed,
    obs_weight,
    noise_field,
    step_sizes,
    lift_weight,
    conv_weights,
    out_weight,
):
    current = prior_state
    for update in range(noise_field.shape[0]):
        step_size = step_sizes[update]
        score = score_all(current, lift_weight, conv_weights, out_weight)
        current = (
            current
            + step_size * (score + obs_weight * (observed - current))
            + jnp.sqrt(2.0 * step_size) * noise_field[update]
        )
    return current


def solution(mesh):
    placed = (
        P(("groups", "tm"), None, "lat", "lon"),
        P(("groups", "tm"), None, "lat", "lon"),
        P(("groups", "tm"), None, "lat", "lon"),
        P(None, ("groups", "tm"), None, "lat", "lon"),
        P(),
        P(),
        P(),
        P(),
    )
    return jax.shard_map(
        per_device,
        mesh=mesh,
        in_specs=placed,
        out_specs=P(("groups", "tm"), None, "lat", "lon"),
        check_vma=False,
    )
```

profile of v0, /device:TPU:0, one launch (start us, length us, event | category | flops | bytes accessed | tf_op | source)
XLA Modules:
  0.0 66.9 jit_solution(1176170069174629272)
XLA Ops:
  0.0 0.9 %copy.89 = f32[2,8,8,128]{3,1,2,0:T(8,128)S(1)} copy(f32[2,8,8,128]{3,2,1,0:T(8,128)} %param.8) | data formatting | bytes 131072 | tf_op args[0]
  0.9 4.9 %collective-permute-start = (f32[2,8,8,128]{3,1,2,0:T(8,128)S(1)}, f32[2,8,8,128]{3,1,2,0:T(8,128)S(1)}, u32[]{:S(2)}, u32[]{:S(2)}) collective-permute-start(f32[2,8,8,128]{3,1,2,0:T(8,128)S(1)} %copy.89), channel_id=1, source_target_pairs={{0,4},{4,8},{8,12},{1,5},{5,9},{9,13},{2,6},{6,10},{10,14},{3,7},{... | collective-permute-start | bytes 196616 | tf_op jit(solution)/shard_map/ppermute | solution.py:14
  5.8 1.3 %collective-permute-start.1 = (f32[2,8,8,128]{3,1,2,0:T(8,128)S(1)}, f32[2,8,8,128]{3,1,2,0:T(8,128)S(1)}, u32[]{:S(2)}, u32[]{:S(2)}) collective-permute-start(f32[2,8,8,128]{3,1,2,0:T(8,128)S(1)} %copy.89), channel_id=1, source_target_pairs={{4,0},{8,4},{12,8},{5,1},{9,5},{13,9},{6,2},{10,6},{14,10},{7,3},{... | collective-permute-start | bytes 196616 | tf_op jit(solution)/shard_map/ppermute | solution.py:17
  7.1 0.9 %fusion.158 = (f32[1,2,8,8,128]{4,3,2,1,0:T(8,128)S(1)}, f32[1,2,8,8,128]{4,3,2,1,0:T(8,128)S(1)}) fusion(f32[2,2,8,8,128]{4,3,2,1,0:T(8,128)} %param.11), kind=kLoop, calls=%fused_computation.204 | loop fusion | bytes 262144 | tf_op jit(solution)/shard_map/slice | solution.py:84
  8.0 1.3 %fusion.159 = (f32[1]{0:T(128)}, f32[1]{0:T(128)}) fusion(f32[2]{0:T(128)} %param.12), kind=kLoop, calls=%fused_computation.205 | loop fusion | bytes 16 | tf_op jit(solution)/shard_map/slice | solution.py:79
  9.3 0.9 %constant_dynamic-update-slice_fusion.1 = f32[2,40,8,128]{3,1,2,0:T(8,128)S(1)} fusion(f32[2,40,8,128]{3,1,2,0:T(8,128)S(1)} %fusion.69, f32[2,8,8,128]{3,2,1,0:T(8,128)} %param.8), kind=kLoop, calls=%fused_computation.151 | loop fusion | bytes 131072
  10.2 1.8 %collective-permute-done.1 = f32[2,8,8,128]{3,1,2,0:T(8,128)S(1)} collective-permute-done((f32[2,8,8,128]{3,1,2,0:T(8,128)S(1)}, f32[2,8,8,128]{3,1,2,0:T(8,128)S(1)}, u32[]{:S(2)}, u32[]{:S(2)}) %collective-permute-start.1) | collective-permute-done | bytes 65568 | tf_op jit(solution)/shard_map/ppermute | solution.py:17
  12.8 1.6 %collective-permute-start.2 = (bf16[2,96,2,128]{3,1,2,0:T(8,128)(2,1)S(1)}, bf16[2,96,2,128]{3,1,2,0:T(8,128)(2,1)S(1)}, u32[]{:S(2)}, u32[]{:S(2)}) collective-permute-start(bf16[2,96,2,128]{3,1,2,0:T(8,128)(2,1)S(1)} %get-tuple-element.11), channel_id=1, source_target_pairs={{0,2},{2,0},{1,3},{3,1},{4,6},{6,4},{5,7},{7,5},{8,10},{10,8},{9,1... | collective-permute-start | bytes 294920 | tf_op jit(solution)/shard_map/ppermute | solution.py:14
  14.9 2.6 %collective-permute-done.2 = bf16[2,96,2,128]{3,1,2,0:T(8,128)(2,1)S(1)} collective-permute-done((bf16[2,96,2,128]{3,1,2,0:T(8,128)(2,1)S(1)}, bf16[2,96,2,128]{3,1,2,0:T(8,128)(2,1)S(1)}, u32[]{:S(2)}, u32[]{:S(2)}) %collective-permute-start.2) | collective-permute-done | bytes 98336 | tf_op jit(solution)/shard_map/ppermute | solution.py:14
  17.5 1.5 %collective-permute-done.3 = bf16[2,96,2,128]{3,1,2,0:T(8,128)(2,1)S(1)} collective-permute-done((bf16[2,96,2,128]{3,1,2,0:T(8,128)(2,1)S(1)}, bf16[2,96,2,128]{3,1,2,0:T(8,128)(2,1)S(1)}, u32[]{:S(2)}, u32[]{:S(2)}) %collective-permute-start.3) | collective-permute-done | bytes 98336 | tf_op jit(solution)/shard_map/ppermute | solution.py:17
  23.5 1.0 %convolution_add_fusion.15 = f32[2,10,130,96]{3,2,1,0:T(8,128)S(1)} fusion(f32[2,10,130,96]{3,2,1,0:T(8,128)S(1)} %fusion.34, bf16[2,96,12,132]{3,1,2,0:T(8,128)(2,1)S(1)} %maximum_multiply_fusion, bf16[2,9,96,96]{3,2,1,0:T(8,128)(2,1)S(1)} %copy-done.1), kind=kOutput, calls=%fused_computation.17 | convolution fusion | flops 48172800 | bytes 3398656 | tf_op jit(solution)/shard_map/oi,firw->forw/dot_general | solution.py:38
  24.4 1.0 %convolution_add_fusion.14 = f32[2,10,130,96]{3,2,1,0:T(8,128)S(1)} fusion(f32[2,10,130,96]{3,2,1,0:T(8,128)S(1)} %convolution_add_fusion.15, bf16[2,96,12,132]{3,1,2,0:T(8,128)(2,1)S(1)} %maximum_multiply_fusion, bf16[2,9,96,96]{3,2,1,0:T(8,128)(2,1)S(1)} %copy-done.1), kind=kOutput, calls=%fused_computation.16 | convolution fusion | flops 48172800 | bytes 3398656 | tf_op jit(solution)/shard_map/oi,firw->forw/dot_general | solution.py:38
  26.0 1.0 %convolution_add_fusion.12 = f32[2,10,130,96]{3,2,1,0:T(8,128)S(1)} fusion(f32[2,10,130,96]{3,2,1,0:T(8,128)S(1)} %convolution_add_fusion.13, bf16[2,96,12,132]{3,1,2,0:T(8,128)(2,1)S(1)} %maximum_multiply_fusion, bf16[2,9,96,96]{3,2,1,0:T(8,128)(2,1)S(1)} %copy-done.1), kind=kOutput, calls=%fused_computation.14 | convolution fusion | flops 48172800 | bytes 3398656 | tf_op jit(solution)/shard_map/oi,firw->forw/dot_general | solution.py:38
  26.9 1.0 %convolution_add_fusion.11 = f32[2,10,130,96]{3,2,1,0:T(8,128)S(1)} fusion(f32[2,10,130,96]{3,2,1,0:T(8,128)S(1)} %convolution_add_fusion.12, bf16[2,96,12,132]{3,1,2,0:T(8,128)(2,1)S(1)} %maximum_multiply_fusion, bf16[2,9,96,96]{3,2,1,0:T(8,128)(2,1)S(1)} %copy-done.1), kind=kOutput, calls=%fused_computation.13 | convolution fusion | flops 48172800 | bytes 3398656 | tf_op jit(solution)/shard_map/oi,firw->forw/dot_general | solution.py:38
  28.5 1.0 %convolution_add_fusion.9 = f32[2,10,130,96]{3,2,1,0:T(8,128)S(1)} fusion(f32[2,10,130,96]{3,2,1,0:T(8,128)S(1)} %convolution_add_fusion.10, bf16[2,96,12,132]{3,1,2,0:T(8,128)(2,1)S(1)} %maximum_multiply_fusion, bf16[2,9,96,96]{3,2,1,0:T(8,128)(2,1)S(1)} %copy-done.1), kind=kOutput, calls=%fused_computation.11 | convolution fusion | flops 48172800 | bytes 3398656 | tf_op jit(solution)/shard_map/oi,firw->forw/dot_general | solution.py:38
  29.4 1.0 %fusion.6 = bf16[2,96,10,130]{1,3,2,0:T(8,128)(2,1)S(1)} fusion(f32[2,10,130,96]{3,2,1,0:T(8,128)S(1)} %convolution_add_fusion.9, bf16[2,96,12,132]{3,1,2,0:T(8,128)(2,1)S(1)} %maximum_multiply_fusion, bf16[10]{0:T(256)(128)(2,1)S(1)} %and_convert_fusion, bf16[2,9,96,96]{3,2,1,0:T(8,128)(2,1)S(1)} %copy-done.1), kind=kOutput, calls=%fused_computation.42 | convolution fusion | flops 49670400 | bytes 2899968 | tf_op jit(solution)/shard_map/oi,firw->forw/dot_general | solution.py:38
  33.6 1.2 %fusion.14 = f32[2,8,8,128]{3,1,2,0:T(8,128)S(1)} fusion(bf16[2,96,8,128]{3,1,2,0:T(8,128)(2,1)S(1)} %fusion.4, f32[2,8,128,96]{2,3,1,0:T(8,128)S(1)} %convolution_add_fusion.25, bf16[2,96,10,130]{1,3,2,0:T(8,128)(2,1)S(1)} %fusion.6, f32[1,2,8,8,128]{4,3,2,1,0:T(8,128)S(1)} %get-tuple-element.14, f32[2,8,8,128]{3,2,1,0:T(8,128)S(1)} %copy-done.3, ...), kind=kOutput, calls=%fused_computation.54 | convolution fusion | flops 42582016 | bytes 2058248 | tf_op jit(solution)/shard_map/co,forw->fcrw/dot_general | solution.py:64
  34.8 3.7 %collective-permute-start.6 = (f32[2,8,8,128]{3,1,2,0:T(8,128)S(1)}, f32[2,8,8,128]{3,1,2,0:T(8,128)S(1)}, u32[]{:S(2)}, u32[]{:S(2)}) collective-permute-start(f32[2,8,8,128]{3,1,2,0:T(8,128)S(1)} %fusion.14), channel_id=1, source_target_pairs={{0,4},{4,8},{8,12},{1,5},{5,9},{9,13},{2,6},{6,10},{10,14},{3,7},{... | collective-permute-start | bytes 196616 | tf_op jit(solution)/shard_map/ppermute | solution.py:14
  38.4 1.3 %collective-permute-start.7 = (f32[2,8,8,128]{3,1,2,0:T(8,128)S(1)}, f32[2,8,8,128]{3,1,2,0:T(8,128)S(1)}, u32[]{:S(2)}, u32[]{:S(2)}) collective-permute-start(f32[2,8,8,128]{3,1,2,0:T(8,128)S(1)} %fusion.14), channel_id=1, source_target_pairs={{4,0},{8,4},{12,8},{5,1},{9,5},{13,9},{6,2},{10,6},{14,10},{7,3},{... | collective-permute-start | bytes 196616 | tf_op jit(solution)/shard_map/ppermute | solution.py:17
  40.4 4.2 %collective-permute-done.7 = f32[2,8,8,128]{3,1,2,0:T(8,128)S(1)} collective-permute-done((f32[2,8,8,128]{3,1,2,0:T(8,128)S(1)}, f32[2,8,8,128]{3,1,2,0:T(8,128)S(1)}, u32[]{:S(2)}, u32[]{:S(2)}) %collective-permute-start.7) | collective-permute-done | bytes 65568 | tf_op jit(solution)/shard_map/ppermute | solution.py:17
  45.5 1.1 %collective-permute-start.8 = (bf16[2,96,2,128]{3,1,2,0:T(8,128)(2,1)S(1)}, bf16[2,96,2,128]{3,1,2,0:T(8,128)(2,1)S(1)}, u32[]{:S(2)}, u32[]{:S(2)}) collective-permute-start(bf16[2,96,2,128]{3,1,2,0:T(8,128)(2,1)S(1)} %get-tuple-element.9), channel_id=1, source_target_pairs={{0,2},{2,0},{1,3},{3,1},{4,6},{6,4},{5,7},{7,5},{8,10},{10,8},{9,1... | collective-permute-start | bytes 294920 | tf_op jit(solution)/shard_map/ppermute | solution.py:14
  46.6 1.0 %collective-permute-start.9 = (bf16[2,96,2,128]{3,1,2,0:T(8,128)(2,1)S(1)}, bf16[2,96,2,128]{3,1,2,0:T(8,128)(2,1)S(1)}, u32[]{:S(2)}, u32[]{:S(2)}) collective-permute-start(bf16[2,96,2,128]{3,1,2,0:T(8,128)(2,1)S(1)} %get-tuple-element.10), channel_id=1, source_target_pairs={{2,0},{0,2},{3,1},{1,3},{6,4},{4,6},{7,5},{5,7},{10,8},{8,10},{11,... | collective-permute-start | bytes 294920 | tf_op jit(solution)/shard_map/ppermute | solution.py:17
  47.6 2.6 %collective-permute-done.8 = bf16[2,96,2,128]{3,1,2,0:T(8,128)(2,1)S(1)} collective-permute-done((bf16[2,96,2,128]{3,1,2,0:T(8,128)(2,1)S(1)}, bf16[2,96,2,128]{3,1,2,0:T(8,128)(2,1)S(1)}, u32[]{:S(2)}, u32[]{:S(2)}) %collective-permute-start.8) | collective-permute-done | bytes 98336 | tf_op jit(solution)/shard_map/ppermute | solution.py:14
  50.2 1.1 %collective-permute-done.9 = bf16[2,96,2,128]{3,1,2,0:T(8,128)(2,1)S(1)} collective-permute-done((bf16[2,96,2,128]{3,1,2,0:T(8,128)(2,1)S(1)}, bf16[2,96,2,128]{3,1,2,0:T(8,128)(2,1)S(1)}, u32[]{:S(2)}, u32[]{:S(2)}) %collective-permute-start.9) | collective-permute-done | bytes 98336 | tf_op jit(solution)/shard_map/ppermute | solution.py:17
  54.1 0.8 %maximum_multiply_fusion.1 = bf16[2,96,12,132]{3,1,2,0:T(8,128)(2,1)S(1)} fusion(bf16[2,96,12,2]{3,1,2,0:T(8,128)(2,1)S(1)} %copy.94, bf16[2,96,2,128]{3,1,2,0:T(8,128)(2,1)S(1)} %collective-permute-done.9, bf16[2,96,8,128]{3,1,2,0:T(8,128)(2,1)S(1)} %fusion.5, bf16[2,96,2,128]{3,1,2,0:T(8,128)(2,1)S(1)} %collective-permute-done.8, ...), kind=kLoop, calls=%fused_computation.45 | loop fusion | flops 3649536 | bytes 1216536 | tf_op jit(solution)/shard_map/mul | solution.py:28
  55.5 1.0 %convolution_add_fusion.7 = f32[2,10,130,96]{3,2,1,0:T(8,128)S(1)} fusion(f32[2,10,130,96]{3,2,1,0:T(8,128)S(1)} %fusion.24, bf16[2,96,12,132]{3,1,2,0:T(8,128)(2,1)S(1)} %maximum_multiply_fusion.1, bf16[2,9,96,96]{3,2,1,0:T(8,128)(2,1)S(1)} %copy-done.1), kind=kOutput, calls=%fused_computation.8 | convolution fusion | flops 48172800 | bytes 3398656 | tf_op jit(solution)/shard_map/oi,firw->forw/dot_general | solution.py:38
  56.5 1.0 %convolution_add_fusion.6 = f32[2,10,130,96]{3,2,1,0:T(8,128)S(1)} fusion(f32[2,10,130,96]{3,2,1,0:T(8,128)S(1)} %convolution_add_fusion.7, bf16[2,96,12,132]{3,1,2,0:T(8,128)(2,1)S(1)} %maximum_multiply_fusion.1, bf16[2,9,96,96]{3,2,1,0:T(8,128)(2,1)S(1)} %copy-done.1), kind=kOutput, calls=%fused_computation.7 | convolution fusion | flops 48172800 | bytes 3398656 | tf_op jit(solution)/shard_map/oi,firw->forw/dot_general | solution.py:38
  58.0 1.0 %convolution_add_fusion.4 = f32[2,10,130,96]{3,2,1,0:T(8,128)S(1)} fusion(f32[2,10,130,96]{3,2,1,0:T(8,128)S(1)} %convolution_add_fusion.5, bf16[2,96,12,132]{3,1,2,0:T(8,128)(2,1)S(1)} %maximum_multiply_fusion.1, bf16[2,9,96,96]{3,2,1,0:T(8,128)(2,1)S(1)} %copy-done.1), kind=kOutput, calls=%fused_computation.5 | convolution fusion | flops 48172800 | bytes 3398656 | tf_op jit(solution)/shard_map/oi,firw->forw/dot_general | solution.py:38
  59.0 1.0 %convolution_add_fusion.3 = f32[2,10,130,96]{3,2,1,0:T(8,128)S(1)} fusion(f32[2,10,130,96]{3,2,1,0:T(8,128)S(1)} %convolution_add_fusion.4, bf16[2,96,12,132]{3,1,2,0:T(8,128)(2,1)S(1)} %maximum_multiply_fusion.1, bf16[2,9,96,96]{3,2,1,0:T(8,128)(2,1)S(1)} %copy-done.1), kind=kOutput, calls=%fused_computation.4 | convolution fusion | flops 48172800 | bytes 3398656 | tf_op jit(solution)/shard_map/oi,firw->forw/dot_general | solution.py:38
  60.5 1.0 %convolution_add_fusion.1 = f32[2,10,130,96]{3,2,1,0:T(8,128)S(1)} fusion(f32[2,10,130,96]{3,2,1,0:T(8,128)S(1)} %convolution_add_fusion.2, bf16[2,96,12,132]{3,1,2,0:T(8,128)(2,1)S(1)} %maximum_multiply_fusion.1, bf16[2,9,96,96]{3,2,1,0:T(8,128)(2,1)S(1)} %copy-done.1), kind=kOutput, calls=%fused_computation.2 | convolution fusion | flops 48172800 | bytes 3398656 | tf_op jit(solution)/shard_map/oi,firw->forw/dot_general | solution.py:38
  61.5 1.0 %fusion.7 = bf16[2,96,10,130]{1,3,2,0:T(8,128)(2,1)S(1)} fusion(f32[2,10,130,96]{3,2,1,0:T(8,128)S(1)} %convolution_add_fusion.1, bf16[2,96,12,132]{3,1,2,0:T(8,128)(2,1)S(1)} %maximum_multiply_fusion.1, bf16[10]{0:T(256)(128)(2,1)S(1)} %and_convert_fusion, bf16[2,9,96,96]{3,2,1,0:T(8,128)(2,1)S(1)} %copy-done.1), kind=kOutput, calls=%fused_computation.43 | convolution fusion | flops 49670400 | bytes 2899968 | tf_op jit(solution)/shard_map/oi,firw->forw/dot_general | solution.py:38
  65.0 1.2 %fusion.15 = f32[2,8,8,128]{3,1,2,0:T(8,128)S(1)} fusion(f32[2,8,8,128]{3,1,2,0:T(8,128)S(1)} %fusion.14, bf16[2,96,8,128]{3,1,2,0:T(8,128)(2,1)S(1)} %fusion.5, f32[2,8,128,96]{2,3,1,0:T(8,128)S(1)} %convolution_add_fusion.17, bf16[2,96,10,130]{1,3,2,0:T(8,128)(2,1)S(1)} %fusion.7, f32[1,2,8,8,128]{4,3,2,1,0:T(8,128)S(1)} %get-tuple-element.13, ...), kind=kOutput, calls=%fused_computation.55 | convolution fusion | flops 42582016 | bytes 2058248 | tf_op jit(solution)/shard_map/co,forw->fcrw/dot_general | solution.py:64
  (74 shorter events, 17.8 us)
Async XLA Ops:
  0.0 12.0 %copy-start = (f32[96,40]{0,1:T(8,128)S(1)}, f32[96,40]{0,1:T(8,128)}, u32[]{:S(2)}) copy-start(f32[96,40]{0,1:T(8,128)} %param.13) | copy-start | bytes 46084
  0.9 8.5 %collective-permute-start = (f32[2,8,8,128]{3,1,2,0:T(8,128)S(1)}, f32[2,8,8,128]{3,1,2,0:T(8,128)S(1)}, u32[]{:S(2)}, u32[]{:S(2)}) collective-permute-start(f32[2,8,8,128]{3,1,2,0:T(8,128)S(1)} %copy.89), channel_id=1, source_target_pairs={{0,4},{4,8},{8,12},{1,5},{5,9},{9,13},{2,6},{6,10},{10,14},{3,7},{... | collective-permute-start | bytes 196616 | tf_op jit(solution)/shard_map/ppermute | solution.py:14
  5.8 6.2 %collective-permute-start.1 = (f32[2,8,8,128]{3,1,2,0:T(8,128)S(1)}, f32[2,8,8,128]{3,1,2,0:T(8,128)S(1)}, u32[]{:S(2)}, u32[]{:S(2)}) collective-permute-start(f32[2,8,8,128]{3,1,2,0:T(8,128)S(1)} %copy.89), channel_id=1, source_target_pairs={{4,0},{8,4},{12,8},{5,1},{9,5},{13,9},{6,2},{10,6},{14,10},{7,3},{... | collective-permute-start | bytes 196616 | tf_op jit(solution)/shard_map/ppermute | solution.py:17
  12.8 4.7 %collective-permute-start.2 = (bf16[2,96,2,128]{3,1,2,0:T(8,128)(2,1)S(1)}, bf16[2,96,2,128]{3,1,2,0:T(8,128)(2,1)S(1)}, u32[]{:S(2)}, u32[]{:S(2)}) collective-permute-start(bf16[2,96,2,128]{3,1,2,0:T(8,128)(2,1)S(1)} %get-tuple-element.11), channel_id=1, source_target_pairs={{0,2},{2,0},{1,3},{3,1},{4,6},{6,4},{5,7},{7,5},{8,10},{10,8},{9,1... | collective-permute-start | bytes 294920 | tf_op jit(solution)/shard_map/ppermute | solution.py:14
  14.4 4.6 %collective-permute-start.3 = (bf16[2,96,2,128]{3,1,2,0:T(8,128)(2,1)S(1)}, bf16[2,96,2,128]{3,1,2,0:T(8,128)(2,1)S(1)}, u32[]{:S(2)}, u32[]{:S(2)}) collective-permute-start(bf16[2,96,2,128]{3,1,2,0:T(8,128)(2,1)S(1)} %get-tuple-element.12), channel_id=1, source_target_pairs={{2,0},{0,2},{3,1},{1,3},{6,4},{4,6},{7,5},{5,7},{10,8},{8,10},{11,... | collective-permute-start | bytes 294920 | tf_op jit(solution)/shard_map/ppermute | solution.py:17
  19.6 1.5 %collective-permute-start.4 = (bf16[2,96,12,2]{1,3,2,0:T(2,128)(2,1)S(1)}, bf16[2,96,12,2]{1,3,2,0:T(2,128)(2,1)S(1)}, u32[]{:S(2)}, u32[]{:S(2)}) collective-permute-start(bf16[2,96,12,2]{1,3,2,0:T(2,128)(2,1)S(1)} %copy.64), channel_id=1, source_target_pairs={{0,1},{1,0},{2,3},{3,2},{4,5},{5,4},{6,7},{7,6},{8,9},{9,8},{10,11... | collective-permute-start | bytes 27656 | tf_op jit(solution)/shard_map/ppermute | solution.py:14
  19.9 1.6 %collective-permute-start.5 = (bf16[2,96,12,2]{1,3,2,0:T(2,128)(2,1)S(1)}, bf16[2,96,12,2]{1,3,2,0:T(2,128)(2,1)S(1)}, u32[]{:S(2)}, u32[]{:S(2)}) collective-permute-start(bf16[2,96,12,2]{1,3,2,0:T(2,128)(2,1)S(1)} %copy.65), channel_id=1, source_target_pairs={{1,0},{0,1},{3,2},{2,3},{5,4},{4,5},{7,6},{6,7},{9,8},{8,9},{11,10... | collective-permute-start | bytes 27656 | tf_op jit(solution)/shard_map/ppermute | solution.py:17
  21.9 1.0 %copy-start.1 = (bf16[2,9,96,96]{3,2,1,0:T(8,128)(2,1)S(1)}, bf16[2,9,96,96]{3,2,1,0:T(8,128)(2,1)}, u32[]{:S(2)}) copy-start(bf16[2,9,96,96]{3,2,1,0:T(8,128)(2,1)} %param.14) | copy-start | bytes 995332
  32.7 0.8 %copy-start.2 = (f32[2,8,8,128]{3,2,1,0:T(8,128)S(1)}, f32[2,8,8,128]{3,2,1,0:T(8,128)}, u32[]{:S(2)}) copy-start(f32[2,8,8,128]{3,2,1,0:T(8,128)} %param.8) | copy-start | bytes 196612
  32.7 0.9 %copy-start.3 = (f32[2,8,8,128]{3,2,1,0:T(8,128)S(1)}, f32[2,8,8,128]{3,2,1,0:T(8,128)}, u32[]{:S(2)}) copy-start(f32[2,8,8,128]{3,2,1,0:T(8,128)} %param.10) | copy-start | bytes 196612
  32.7 0.9 %copy-start.4 = (f32[2,8,8,128]{3,2,1,0:T(8,128)S(1)}, f32[2,8,8,128]{3,2,1,0:T(8,128)}, u32[]{:S(2)}) copy-start(f32[2,8,8,128]{3,2,1,0:T(8,128)} %param.9) | copy-start | bytes 196612
  32.7 0.9 %copy-start.5 = (bf16[8,96]{1,0:T(8,128)(2,1)S(1)}, bf16[8,96]{1,0:T(8,128)(2,1)}, u32[]{:S(2)}) copy-start(bf16[8,96]{1,0:T(8,128)(2,1)} %param.15) | copy-start | bytes 4612
  34.8 5.5 %collective-permute-start.6 = (f32[2,8,8,128]{3,1,2,0:T(8,128)S(1)}, f32[2,8,8,128]{3,1,2,0:T(8,128)S(1)}, u32[]{:S(2)}, u32[]{:S(2)}) collective-permute-start(f32[2,8,8,128]{3,1,2,0:T(8,128)S(1)} %fusion.14), channel_id=1, source_target_pairs={{0,4},{4,8},{8,12},{1,5},{5,9},{9,13},{2,6},{6,10},{10,14},{3,7},{... | collective-permute-start | bytes 196616 | tf_op jit(solution)/shard_map/ppermute | solution.py:14
  38.4 6.2 %collective-permute-start.7 = (f32[2,8,8,128]{3,1,2,0:T(8,128)S(1)}, f32[2,8,8,128]{3,1,2,0:T(8,128)S(1)}, u32[]{:S(2)}, u32[]{:S(2)}) collective-permute-start(f32[2,8,8,128]{3,1,2,0:T(8,128)S(1)} %fusion.14), channel_id=1, source_target_pairs={{4,0},{8,4},{12,8},{5,1},{9,5},{13,9},{6,2},{10,6},{14,10},{7,3},{... | collective-permute-start | bytes 196616 | tf_op jit(solution)/shard_map/ppermute | solution.py:17
  45.5 4.7 %collective-permute-start.8 = (bf16[2,96,2,128]{3,1,2,0:T(8,128)(2,1)S(1)}, bf16[2,96,2,128]{3,1,2,0:T(8,128)(2,1)S(1)}, u32[]{:S(2)}, u32[]{:S(2)}) collective-permute-start(bf16[2,96,2,128]{3,1,2,0:T(8,128)(2,1)S(1)} %get-tuple-element.9), channel_id=1, source_target_pairs={{0,2},{2,0},{1,3},{3,1},{4,6},{6,4},{5,7},{7,5},{8,10},{10,8},{9,1... | collective-permute-start | bytes 294920 | tf_op jit(solution)/shard_map/ppermute | solution.py:14
  46.6 4.6 %collective-permute-start.9 = (bf16[2,96,2,128]{3,1,2,0:T(8,128)(2,1)S(1)}, bf16[2,96,2,128]{3,1,2,0:T(8,128)(2,1)S(1)}, u32[]{:S(2)}, u32[]{:S(2)}) collective-permute-start(bf16[2,96,2,128]{3,1,2,0:T(8,128)(2,1)S(1)} %get-tuple-element.10), channel_id=1, source_target_pairs={{2,0},{0,2},{3,1},{1,3},{6,4},{4,6},{7,5},{5,7},{10,8},{8,10},{11,... | collective-permute-start | bytes 294920 | tf_op jit(solution)/shard_map/ppermute | solution.py:17
  51.8 1.6 %collective-permute-start.10 = (bf16[2,96,12,2]{1,3,2,0:T(2,128)(2,1)S(1)}, bf16[2,96,12,2]{1,3,2,0:T(2,128)(2,1)S(1)}, u32[]{:S(2)}, u32[]{:S(2)}) collective-permute-start(bf16[2,96,12,2]{1,3,2,0:T(2,128)(2,1)S(1)} %copy.91), channel_id=1, source_target_pairs={{0,1},{1,0},{2,3},{3,2},{4,5},{5,4},{6,7},{7,6},{8,9},{9,8},{10,11... | collective-permute-start | bytes 27656 | tf_op jit(solution)/shard_map/ppermute | solution.py:14
  52.1 1.6 %collective-permute-start.11 = (bf16[2,96,12,2]{1,3,2,0:T(2,128)(2,1)S(1)}, bf16[2,96,12,2]{1,3,2,0:T(2,128)(2,1)S(1)}, u32[]{:S(2)}, u32[]{:S(2)}) collective-permute-start(bf16[2,96,12,2]{1,3,2,0:T(2,128)(2,1)S(1)} %copy.92), channel_id=1, source_target_pairs={{1,0},{0,1},{3,2},{2,3},{5,4},{4,5},{7,6},{6,7},{9,8},{8,9},{11,10... | collective-permute-start | bytes 27656 | tf_op jit(solution)/shard_map/ppermute | solution.py:17
where the time goes:
time: 67.4 us; the launch traced here: 66.9 us
  matrix products  24.1 us (36%)
  starting transfers between devices  16.5 us (24%)
  waiting for transfers between devices  14.3 us (21%)
  local copies, waits for them, and re-layouts  8.35 us (12%)
  other arithmetic  1.85 us (3%)
  between operations  1.72 us (3%)
    dot_general x34, matrix products, conv_valid(): jnp.einsum('oi,firw->forw', kernel[3 * row_off + col_off], part, preferre...  20.1 us
    ppermute x6, starting transfers between devices, extended_2(): lax.ppermute(lax.slice_in_dim(block, block.shape[dim] - width, None, axis...  11.4 us
    ppermute x6, waiting for transfers between devices, extended_2(): lax.ppermute(lax.slice_in_dim(block, 0, width, axis=dim), axis, backward)  8.56 us
    ppermute x6, waiting for transfers between devices, extended_2(): lax.ppermute(lax.slice_in_dim(block, block.shape[dim] - width, None, axis...  5.77 us
    ppermute x6, starting transfers between devices, extended_2(): lax.ppermute(lax.slice_in_dim(block, 0, width, axis=dim), axis, backward)  5.17 us
    unnamed x17, local copies, waits for them, and re-layouts  2.48 us
    dot_general x2, matrix products, score_all(): jnp.einsum('co,forw->fcrw', out_weight, merged, preferred_element_type=jn...  2.39 us
    mul x2, other arithmetic, rim_rows(): return values * inside.astype(values.dtype)[None, None, :, None]  1.67 us
  transfers between devices with their start and end apart: 12, of which 7 were waited for; matrix products, arithmetic and copies ran while one was open for 7% of the time, Pallas kernels for 0%

commit v1 on v0

v1 whole, which is shorter than its diff:
```python
import functools

import jax
import jax.numpy as jnp
from jax import lax
from jax.experimental import pallas as pl
from jax.experimental.pallas import tpu as pltpu
from jax.sharding import PartitionSpec as P

F32 = jnp.float32
BF16 = jnp.bfloat16
LANES = 128
GUARD = 8


def silu(value):
    half = 0.5 * value
    return half + half * jnp.tanh(half)


def transposed(matrix):
    return jnp.transpose(matrix.astype(F32))


def kernel(
    dims,
    steps_ref,
    prior_hbm,
    observed_hbm,
    obs_weight_hbm,
    noise_hbm,
    lift_hbm,
    conv_hbm,
    out_weight_hbm,
    result_ref,
    prior,
    observed,
    obs_weight,
    noise,
    lift_in,
    conv_in,
    out_in,
    load_sem,
    send_sem,
    recv_sem,
    state,
    main,
    edge_out,
    edge_in,
    lift_f32,
    lift_w,
    conv_w,
    out_f32,
    out_w,
    lifted,
    lifted_cols,
    activated,
    activated_cols,
):
    frames, chans, rows, cols, hidden, updates, margin = dims
    tile = frames * chans
    group = cols // rows
    span = rows + 2 * margin
    wide = cols + 2 * GUARD
    t, t_size = lax.axis_index("tm"), lax.axis_size("tm")
    l, l_size = lax.axis_index("lat"), lax.axis_size("lat")
    other = lax.rem(lax.axis_index("lon") + 1, lax.axis_size("lon"))

    loads = [
        pltpu.make_async_copy(source, target, load_sem.at[index])
        for index, (source, target) in enumerate(
            (
                (prior_hbm, prior),
                (conv_hbm, conv_in),
                (lift_hbm, lift_in),
                (out_weight_hbm, out_in),
                (observed_hbm, observed),
                (obs_weight_hbm, obs_weight),
                (noise_hbm, noise),
            )
        )
    ]
    for load in loads:
        load.start()

    main[...] = jnp.zeros_like(main)
    edge_in[...] = jnp.zeros_like(edge_in)

    around = [
        (dt, dl, do)
        for dt in (-1, 0, 1)
        for dl in (-1, 0, 1)
        for do in (0, 1)
        if (dt, dl, do) != (0, 0, 0)
    ]

    def exists(dt, dl):
        return (t + dt >= 0) & (t + dt < t_size) & (l + dl >= 0) & (l + dl < l_size)

    def target(dt, dl, do):
        own = lax.axis_index("lon")
        return {"tm": t + dt, "lat": l + dl, "lon": other if do else own}

    barrier = pltpu.get_barrier_semaphore()
    for dt, dl, do in around:

        @pl.when(exists(dt, dl))
        def _():
            pl.semaphore_signal(
                barrier, inc=1, device_id=target(dt, dl, do), device_id_type=pl.DeviceIdType.MESH
            )

    def one(flag):
        return flag.astype(jnp.int32)

    t_count = 1 + one(t > 0) + one(t < t_size - 1)
    l_count = 1 + one(l > 0) + one(l < l_size - 1)

    def message(u, dt, dl, do):
        slot, kind = 1 - dt, 1 - dl
        if do:
            source, place = edge_out.at[u], edge_in.at[u, slot, kind]
        elif dl == 0:
            source = main.at[u, 1, pl.ds(margin, rows)]
            place = main.at[u, slot, pl.ds(margin, rows)]
        elif dl == 1:
            source = main.at[u, 1, pl.ds(rows, margin)]
            place = main.at[u, slot, pl.ds(0, margin)]
        else:
            source = main.at[u, 1, pl.ds(margin, margin)]
            place = main.at[u, slot, pl.ds(margin + rows, margin)]
        where = (slot * 3 + kind) * 2 + do
        return pltpu.make_async_remote_copy(
            src_ref=source,
            dst_ref=place,
            send_sem=send_sem.at[u, where],
            recv_sem=recv_sem.at[u, where],
            device_id=target(dt, dl, do),
            device_id_type=pl.DeviceIdType.MESH,
        )

    lane_group = lax.broadcasted_iota(jnp.int32, (tile, cols), 1) // group

    def send_all(u):
        edge = jnp.zeros((tile, cols), F32)
        for row in range(rows):
            value = state[row]
            main[u, 1, margin + row] = value.astype(BF16)
            turned = pltpu.roll(value, (group * row + group // 2) % cols, 1)
            edge = jnp.where(lane_group == row, turned, edge)
        edge_out[u] = edge.astype(BF16)
        if u == 0:
            pl.semaphore_wait(barrier, t_count * l_count * 2 - 1)
        for dt, dl, do in around:

            @pl.when(exists(dt, dl))
            def _():
                message(u, dt, dl, do).start()

    def receive_all(u):
        for dt, dl, do in around:

            @pl.when(exists(-dt, -dl))
            def _():
                message(u, dt, dl, do).wait_recv()

    def strided(frame, row):
        return pl.ds(frame * chans * rows + row, chans, stride=rows)

    loads[0].wait()
    for row in range(rows):
        state[row] = jnp.concatenate(
            [prior[strided(frame, row), :] for frame in range(frames)], axis=0
        )
    send_all(0)

    lift_f32[...] = jnp.zeros_like(lift_f32)
    conv_w[...] = jnp.zeros_like(conv_w)
    out_f32[...] = jnp.zeros_like(out_f32)
    lifted[...] = jnp.zeros_like(lifted)
    for load in loads[1:4]:
        load.wait()
    depth = lift_in.shape[1]
    pile = 3 * tile
    turned = transposed(lift_in[...])
    high = turned.astype(BF16).astype(F32)
    low = turned - high
    for part, value in enumerate((high, low)):
        for frame in range(frames):
            lift_f32[pl.ds(part * pile + frame * chans, depth), pl.ds(frame * LANES, hidden)] = value
    lift_w[...] = lift_f32[...].astype(BF16)
    for layer in range(2):
        for a in range(3):
            for b in range(3):
                tap = transposed(conv_in[layer, 3 * a + b]).astype(BF16)
                for q in range(2):
                    conv_w[
                        layer, pl.ds(((a + q) * 3 + b) * LANES, hidden), pl.ds(q * LANES, hidden)
                    ] = tap
    for q in range(2):
        out_f32[pl.ds(q * chans, chans), pl.ds(q * LANES, hidden)] = out_in[...].astype(F32)
    out_w[...] = out_f32[...].astype(BF16)
    for load in loads[4:]:
        load.wait()

    def lift(values):
        stacked = jnp.concatenate(values + values, axis=0)
        result = lax.dot_general(
            stacked, lift_w[...], (((0,), (0,)), ((), ())), preferred_element_type=F32
        )
        return result.astype(BF16).astype(F32)

    for u in range(updates):
        receive_all(u)

        for row in range(span):
            lifted[row, pl.ds(GUARD, cols)] = lift([main[u, slot, row] for slot in range(3)])
        own_edge = lift([edge_in[u, slot, 1] for slot in range(3)])
        far_edge = lift(
            [
                jnp.where(
                    lane_group < rows // 2,
                    edge_in[u, slot, 2].astype(F32),
                    edge_in[u, slot, 0].astype(F32),
                ).astype(BF16)
                for slot in range(3)
            ]
        )
        for row in range(span):
            if row < margin:
                start, edge = group * (rows - margin + row), far_edge
            elif row < margin + rows:
                start, edge = group * (row - margin), own_edge
            else:
                start, edge = group * (row - margin - rows), far_edge
            middle = start + group // 2
            lifted[row, pl.ds(0, GUARD)] = edge[middle - GUARD : middle]
            lifted[row, pl.ds(GUARD + cols, GUARD)] = edge[middle : middle + GUARD]
        for row in range(span):
            for b in range(3):
                lifted_cols[b, row] = lifted[row, pl.ds(GUARD - 2 + b, wide)].astype(BF16)

        top = jnp.where(l == 0, 0.0, 1.0).astype(F32)
        bottom = jnp.where(l == l_size - 1, 0.0, 1.0).astype(F32)
        pairs = rows // 2 + 1
        for pair in range(pairs):
            for frame in range(frames):
                part = pl.ds(frame * LANES, LANES)
                window = jnp.concatenate(
                    [lifted_cols[b, 2 * pair + r, :, part] for r in range(4) for b in range(3)],
                    axis=1,
                )
                result = silu(jnp.dot(window, conv_w[0], preferred_element_type=F32))
                for q in range(2):
                    value = result[:, q * LANES : (q + 1) * LANES]
                    if pair == 0 and q == 0:
                        value = value * top
                    if pair == pairs - 1 and q == 1:
                        value = value * bottom
                    activated[frame, 2 * pair + q] = value
        for frame in range(frames):
            for row in range(rows + 2):
                for b in range(3):
                    activated_cols[b, frame, row] = activated[frame, row, pl.ds(b, cols)].astype(BF16)

        step = jnp.full((chans, cols), steps_ref[u], F32)
        spread = jnp.sqrt(2.0 * step)
        for pair in range(rows // 2):
            for frame in range(frames):
                part = pl.ds(frame * LANES, LANES)
                window = jnp.concatenate(
                    [activated_cols[b, frame, 2 * pair + r] for r in range(4) for b in range(3)],
                    axis=1,
                )
                second = silu(jnp.dot(window, conv_w[1], preferred_element_type=F32))
                base = jnp.concatenate(
                    [lifted[margin + 2 * pair + q, pl.ds(GUARD, cols), part] for q in range(2)],
                    axis=1,
                )
                merged = (base + second).astype(BF16)
                score = lax.dot_general(
                    out_w[...], merged, (((1,), (1,)), ((), ())), preferred_element_type=F32
                )
                for q in range(2):
                    row = 2 * pair + q
                    own = pl.ds(frame * chans, chans)
                    where = strided(frame, row)
                    current = state[row, own]
                    pull = obs_weight[where, :] * (observed[where, :] - current)
                    fresh = (
                        current
                        + step * (score[q * chans : (q + 1) * chans] + pull)
                        + spread * noise[u, where, :]
                    )
                    if u == updates - 1:
                        result_ref[where, :] = fresh
                    else:
                        state[row, own] = fresh
        if u < updates - 1:
            send_all(u + 1)

    for u in range(updates):
        for dt, dl, do in around:

            @pl.when(exists(dt, dl))
            def _():
                message(u, dt, dl, do).wait_send()


def per_device(
    prior_state, observed, obs_weight, noise_field, step_sizes, lift_weight, conv_weights, out_weight
):
    frames, chans, rows, cols = prior_state.shape
    hidden, depth = lift_weight.shape
    updates = noise_field.shape[0]
    margin = 2
    tile = frames * chans
    span = rows + 2 * margin
    wide = cols + 2 * GUARD
    flat = (tile * rows, cols)
    dims = (frames, chans, rows, cols, hidden, updates, margin)
    vmem = pltpu.VMEM
    result = pl.pallas_call(
        functools.partial(kernel, dims),
        out_shape=jax.ShapeDtypeStruct(flat, F32),
        in_specs=[pl.BlockSpec(memory_space=pltpu.SMEM)] + [pl.BlockSpec(memory_space=pl.ANY)] * 7,
        out_specs=pl.BlockSpec(memory_space=pltpu.VMEM),
        scratch_shapes=[
            vmem(flat, F32),
            vmem(flat, F32),
            vmem(flat, F32),
            vmem((updates, *flat), F32),
            vmem(lift_weight.shape, F32),
            vmem(conv_weights.shape, BF16),
            vmem(out_weight.shape, BF16),
            pltpu.SemaphoreType.DMA((7,)),
            pltpu.SemaphoreType.DMA((updates, 18)),
            pltpu.SemaphoreType.DMA((updates, 18)),
            vmem((rows, tile, cols), F32),
            vmem((updates, 3, span, tile, cols), BF16),
            vmem((updates, tile, cols), BF16),
            vmem((updates, 3, 3, tile, cols), BF16),
            vmem((6 * tile, frames * LANES), F32),
            vmem((6 * tile, frames * LANES), BF16),
            vmem((2, 12 * LANES, 2 * LANES), BF16),
            vmem((2 * chans, 2 * LANES), F32),
            vmem((2 * chans, 2 * LANES), BF16),
            vmem((span, wide + GUARD, frames * LANES), F32),
            vmem((3, span, wide, frames * LANES), BF16),
            vmem((frames, rows + 2, wide, LANES), F32),
            vmem((3, frames, rows + 2, cols, LANES), BF16),
        ],
        compiler_params=pltpu.CompilerParams(
            collective_id=0, has_side_effects=True, vmem_limit_bytes=40 * 1024 * 1024
        ),
        cost_estimate=pl.CostEstimate(
            flops=4 * updates * tile * rows * cols * hidden * 9 * hidden // chans,
            bytes_accessed=1 << 20,
            transcendentals=0,
        ),
    )(
        step_sizes,
        prior_state.reshape(flat),
        observed.reshape(flat),
        obs_weight.reshape(flat),
        noise_field.reshape(updates, *flat),
        lift_weight,
        conv_weights,
        out_weight,
    )
    return result.reshape(prior_state.shape)


def solution(mesh):
    placed = (
        P(("groups", "tm"), None, "lat", "lon"),
        P(("groups", "tm"), None, "lat", "lon"),
        P(("groups", "tm"), None, "lat", "lon"),
        P(None, ("groups", "tm"), None, "lat", "lon"),
        P(),
        P(),
        P(),
        P(),
    )
    return jax.shard_map(
        per_device,
        mesh=mesh,
        in_specs=placed,
        out_specs=P(("groups", "tm"), None, "lat", "lon"),
        check_vma=False,
    )
```

time: 67.4 us -> 28.7 us (0.43)
  matrix products: 24.1 us -> 0 us
  Pallas kernels: 0 us -> 23.3 us
  starting transfers between devices: 16.5 us -> 0 us
  waiting for transfers between devices: 14.3 us -> 0 us
  local copies, waits for them, and re-layouts: 8.35 us -> 5.08 us
  other arithmetic: 1.85 us -> 0 us
  between operations: 1.72 us -> 0.05 us
    dot_general x38 -> x0, matrix products: 24.1 us -> none  [the longest x34 20.1 us: conv_valid(): jnp.einsum('oi,firw->forw', kernel[3 * row_off + col_off], part, preferre...]
    pallas_call x0 -> x1, Pallas kernels: none -> 23.3 us  [per_device(): pl.pallas_call(functools.partial(kernel, dims), out_shape=jax.ShapeDtypeS...]
    ppermute x12 -> x0, starting transfers between devices: 16.5 us -> none  [the longest x6 11.4 us: extended_2(): lax.ppermute(lax.slice_in_dim(block, block.shape[dim] - width, None, axis...]
    ppermute x12 -> x0, waiting for transfers between devices: 14.3 us -> none  [the longest x6 8.56 us: extended_2(): lax.ppermute(lax.slice_in_dim(block, 0, width, axis=dim), axis, backward)]
    slice x10 -> x0, local copies, waits for them, and re-layouts: 3.8 us -> none  [the longest x1 1.31 us: per_device(): step_size = step_sizes[update]]
    unnamed x17 -> x16, local copies, waits for them, and re-layouts: 2.48 us -> 5.08 us
    mul x2 -> x0, other arithmetic: 1.67 us -> none  [rim_rows(): return values * inside.astype(values.dtype)[None, None, :, None]]
    ppermute x4 -> x0, local copies, waits for them, and re-layouts: 1.41 us -> none  [the longest x2 0.71 us: extended_2(): lax.ppermute(lax.slice_in_dim(block, block.shape[dim] - width, None, axis...]
  transfers between devices with their start and end apart: 12 -> 0, of which waited for: 7 -> 0; matrix products, arithmetic and copies ran while one was open for 7% -> 0% of each run, Pallas kernels for 0% -> 0%
where the time goes in v1:
time: 28.7 us; the launch traced here: 28.4 us
  Pallas kernels  23.3 us (81%)
  local copies, waits for them, and re-layouts  5.08 us (18%)
    pallas_call x1, Pallas kernels, per_device(): pl.pallas_call(functools.partial(kernel, dims), out_shape=jax.ShapeDtypeS...  23.3 us
    unnamed x16, local copies, waits for them, and re-layouts  5.08 us

profile of v1, /device:TPU:0, one launch (start us, length us, event | category | flops | bytes accessed | tf_op | source)
XLA Modules:
  0.0 28.4 jit_solution(7748554256751619951)
XLA Ops:
  0.0 0.0 copy-start.2
  0.0 0.0 copy-start.5
  0.0 0.0 copy-start.6
  0.0 0.8 %copy.9.lift_hbm = f32[96,40]{1,0:T(8,128)S(1)} copy(f32[96,40]{0,1:T(8,128)} %param.13) | data formatting | bytes 30720 | tf_op args[5]
  0.9 0.0 copy-done.2
  0.9 0.0 copy-done.5
  0.9 0.0 copy-done.6
  0.9 0.0 copy-start
  0.9 1.0 %copy-done = bf16[2,9,96,96]{3,2,1,0:T(8,128)(2,1)S(1)} copy-done((bf16[2,9,96,96]{3,2,1,0:T(8,128)(2,1)S(1)}, bf16[2,9,96,96]{3,2,1,0:T(8,128)(2,1)}, u32[]{:S(2)}) %copy-start) | copy-done | bytes 331800
  1.9 0.0 copy-start.1
  1.9 0.9 %copy-done.1 = f32[2,2,8,8,128]{4,3,2,1,0:T(8,128)S(1)} copy-done((f32[2,2,8,8,128]{4,3,2,1,0:T(8,128)S(1)}, f32[2,2,8,8,128]{4,3,2,1,0:T(8,128)}, u32[]{:S(2)}) %copy-start.1) | copy-done | bytes 131096
  2.8 0.0 copy-start.3
  2.8 0.8 %copy-done.3 = f32[2,8,8,128]{3,2,1,0:T(8,128)S(1)} copy-done((f32[2,8,8,128]{3,2,1,0:T(8,128)S(1)}, f32[2,8,8,128]{3,2,1,0:T(8,128)}, u32[]{:S(2)}) %copy-start.3) | copy-done | bytes 65560
  3.6 0.0 copy-start.4
  3.6 0.8 %copy-done.4 = f32[2,8,8,128]{3,2,1,0:T(8,128)S(1)} copy-done((f32[2,8,8,128]{3,2,1,0:T(8,128)S(1)}, f32[2,8,8,128]{3,2,1,0:T(8,128)}, u32[]{:S(2)}) %copy-start.4) | copy-done | bytes 65560
  4.5 23.3 %shard_map.82 = f32[128,128]{1,0:T(8,128)S(1)} custom-call(f32[2]{0:T(128)S(1)} %copy-done.6, f32[128,128]{1,0:T(8,128)S(1)} %bitcast.7, f32[128,128]{1,0:T(8,128)S(1)} %bitcast.8, f32[128,128]{1,0:T(8,128)S(1)} %bitcast.9, f32[2,128,128]{2,1,0:T(8,128)S(1)} %bitcast.6, f32[96,40]{1,0:T(8,128)S(1)} %copy.9.lift_hbm, bf16[2,9,96,96]{3,2,1,0:T(8,128)(2,1)S(1)} %copy-done, ...), custom_call_target="tpu_custom_call" | custom-call | flops 1358954496 | bytes 1048576 | tf_op jit(solution)/shard_map/pallas_call | solution.py:323
  27.8 0.6 %copy.11 = f32[2,8,8,128]{3,2,1,0:T(8,128)} copy(f32[2,8,8,128]{3,2,1,0:T(8,128)S(1)} %bitcast.5) | data formatting | bytes 131072
Async XLA Ops:
  0.0 0.9 %copy-start.2 = (f32[2,8,8,128]{3,2,1,0:T(8,128)S(1)}, f32[2,8,8,128]{3,2,1,0:T(8,128)}, u32[]{:S(2)}) copy-start(f32[2,8,8,128]{3,2,1,0:T(8,128)} %param.8) | copy-start | bytes 196612
  0.0 0.9 %copy-start.5 = (bf16[8,96]{1,0:T(8,128)(2,1)S(1)}, bf16[8,96]{1,0:T(8,128)(2,1)}, u32[]{:S(2)}) copy-start(bf16[8,96]{1,0:T(8,128)(2,1)} %out_weight_hbm.1) | copy-start | bytes 4612
  0.0 0.9 %copy-start.6 = (f32[2]{0:T(128)S(1)}, f32[2]{0:T(128)}, u32[]{:S(2)}) copy-start(f32[2]{0:T(128)} %steps_ref.1) | copy-start | bytes 28
  0.9 1.0 %copy-start = (bf16[2,9,96,96]{3,2,1,0:T(8,128)(2,1)S(1)}, bf16[2,9,96,96]{3,2,1,0:T(8,128)(2,1)}, u32[]{:S(2)}) copy-start(bf16[2,9,96,96]{3,2,1,0:T(8,128)(2,1)} %conv_hbm.1) | copy-start | bytes 995332
  1.9 0.9 %copy-start.1 = (f32[2,2,8,8,128]{4,3,2,1,0:T(8,128)S(1)}, f32[2,2,8,8,128]{4,3,2,1,0:T(8,128)}, u32[]{:S(2)}) copy-start(f32[2,2,8,8,128]{4,3,2,1,0:T(8,128)} %param.11) | copy-start | bytes 393220
  2.8 0.8 %copy-start.3 = (f32[2,8,8,128]{3,2,1,0:T(8,128)S(1)}, f32[2,8,8,128]{3,2,1,0:T(8,128)}, u32[]{:S(2)}) copy-start(f32[2,8,8,128]{3,2,1,0:T(8,128)} %param.9) | copy-start | bytes 196612
  3.6 0.8 %copy-start.4 = (f32[2,8,8,128]{3,2,1,0:T(8,128)S(1)}, f32[2,8,8,128]{3,2,1,0:T(8,128)}, u32[]{:S(2)}) copy-start(f32[2,8,8,128]{3,2,1,0:T(8,128)} %param.10) | copy-start | bytes 196612

commit v2 on v1

v2 whole, which is shorter than its diff:
```python
import functools

import jax
import jax.numpy as jnp
from jax import lax
from jax.experimental import pallas as pl
from jax.experimental.pallas import tpu as pltpu
from jax.sharding import PartitionSpec as P

F32 = jnp.float32
BF16 = jnp.bfloat16
LANES = 128
GUARD = 8


def silu(value):
    half = 0.5 * value
    return half + half * jnp.tanh(half)


def transposed(matrix):
    return jnp.transpose(matrix.astype(F32))


def kernel(
    dims,
    steps_ref,
    prior_hbm,
    observed_hbm,
    obs_weight_hbm,
    noise_hbm,
    lift_hbm,
    conv_hbm,
    out_weight_hbm,
    result_ref,
    prior,
    observed,
    obs_weight,
    noise,
    lift_in,
    conv_in,
    out_in,
    load_sem,
    send_sem,
    recv_sem,
    state,
    main,
    edge_out,
    edge_in,
    lift_f32,
    lift_w,
    conv_w,
    out_f32,
    out_w,
    lifted,
    lifted_cols,
    activated,
    activated_cols,
):
    frames, chans, rows, cols, hidden, updates, margin = dims
    tile = frames * chans
    group = cols // rows
    span = rows + 2 * margin
    wide = cols + 2 * GUARD
    t, t_size = lax.axis_index("tm"), lax.axis_size("tm")
    l, l_size = lax.axis_index("lat"), lax.axis_size("lat")
    other = lax.rem(lax.axis_index("lon") + 1, lax.axis_size("lon"))

    loads = [
        pltpu.make_async_copy(source, target, load_sem.at[index])
        for index, (source, target) in enumerate(
            (
                (prior_hbm, prior),
                (conv_hbm, conv_in),
                (lift_hbm, lift_in),
                (out_weight_hbm, out_in),
                (observed_hbm, observed),
                (obs_weight_hbm, obs_weight),
                (noise_hbm, noise),
            )
        )
    ]
    for load in loads:
        load.start()

    main[...] = jnp.zeros_like(main)
    edge_in[...] = jnp.zeros_like(edge_in)

    around = [
        (dt, dl, do)
        for dt in (-1, 0, 1)
        for dl in (-1, 0, 1)
        for do in (0, 1)
        if (dt, dl, do) != (0, 0, 0)
    ]

    def exists(dt, dl):
        return (t + dt >= 0) & (t + dt < t_size) & (l + dl >= 0) & (l + dl < l_size)

    def target(dt, dl, do):
        own = lax.axis_index("lon")
        return {"tm": t + dt, "lat": l + dl, "lon": other if do else own}

    barrier = pltpu.get_barrier_semaphore()
    for dt, dl, do in around:

        @pl.when(exists(dt, dl))
        def _():
            pl.semaphore_signal(
                barrier, inc=1, device_id=target(dt, dl, do), device_id_type=pl.DeviceIdType.MESH
            )

    def one(flag):
        return flag.astype(jnp.int32)

    t_count = 1 + one(t > 0) + one(t < t_size - 1)
    l_count = 1 + one(l > 0) + one(l < l_size - 1)

    def message(u, dt, dl, do, chunk=0):
        slot, kind = 1 - dt, 1 - dl
        first, count = (margin * chunk, margin) if u else (0, rows)
        if do:
            source, place = edge_out.at[u], edge_in.at[u, slot, kind]
        elif dl == 0:
            source = main.at[u, 1, pl.ds(margin + first, count)]
            place = main.at[u, slot, pl.ds(margin + first, count)]
        elif dl == 1:
            source = main.at[u, 1, pl.ds(rows, margin)]
            place = main.at[u, slot, pl.ds(0, margin)]
        else:
            source = main.at[u, 1, pl.ds(margin, margin)]
            place = main.at[u, slot, pl.ds(margin + rows, margin)]
        where = ((slot * 3 + kind) * 2 + do) * (rows // margin) + chunk
        return pltpu.make_async_remote_copy(
            src_ref=source,
            dst_ref=place,
            send_sem=send_sem.at[u, where],
            recv_sem=recv_sem.at[u, where],
            device_id=target(dt, dl, do),
            device_id_type=pl.DeviceIdType.MESH,
        )

    lane_group = lax.broadcasted_iota(jnp.int32, (tile, cols), 1) // group

    def halves(value):
        high = value.astype(BF16)
        return jnp.concatenate([high, (value - high.astype(F32)).astype(BF16)], axis=0)

    def send(u, dt, dl, do, chunk=0):
        @pl.when(exists(dt, dl))
        def _():
            message(u, dt, dl, do, chunk).start()

    def chunks_of(u, dl, do):
        return range(rows // margin) if u and dl == 0 and not do else range(1)

    def keep(u, row, value):
        state[row] = value
        main[u, 1, margin + row] = halves(value)

    def send_chunk(u, chunk):
        for dt in (-1, 1):
            send(u, dt, 0, 0, chunk)
        if chunk == 0:
            for dt in (-1, 0, 1):
                send(u, dt, -1, 0)
        if chunk == rows // margin - 1:
            for dt in (-1, 0, 1):
                send(u, dt, 1, 0)

    def send_edges(u):
        edge = jnp.zeros((tile, cols), F32)
        for row in range(rows):
            turned = pltpu.roll(state[row], (group * row + group // 2) % cols, 1)
            edge = jnp.where(lane_group == row, turned, edge)
        edge_out[u] = halves(edge)
        for dt in (-1, 0, 1):
            for dl in (-1, 0, 1):
                send(u, dt, dl, 1)

    def receive_all(u):
        for dt, dl, do in around:

            @pl.when(exists(-dt, -dl))
            def _():
                for chunk in chunks_of(u, dl, do):
                    message(u, dt, dl, do, chunk).wait_recv()

    def strided(frame, row):
        return pl.ds(frame * chans * rows + row, chans, stride=rows)

    loads[0].wait()
    for row in range(rows):
        keep(
            0,
            row,
            jnp.concatenate([prior[strided(frame, row), :] for frame in range(frames)], axis=0),
        )
    pl.semaphore_wait(barrier, t_count * l_count * 2 - 1)
    for dt in (-1, 1):
        send(0, dt, 0, 0)
    for dt in (-1, 0, 1):
        for dl in (-1, 1):
            send(0, dt, dl, 0)
    send_edges(0)

    lift_f32[...] = jnp.zeros_like(lift_f32)
    conv_w[...] = jnp.zeros_like(conv_w)
    out_f32[...] = jnp.zeros_like(out_f32)
    lifted[...] = jnp.zeros_like(lifted)
    for load in loads[1:4]:
        load.wait()
    depth = lift_in.shape[0]
    turned = lift_in[...]
    high = turned.astype(BF16).astype(F32)
    low = turned - high
    for frame in range(frames):
        part = pl.ds(frame * LANES, hidden)
        for item in range(depth // chans):
            source = slice(item * chans, (item + 1) * chans)
            slot, place = divmod((item + frame) * chans, tile)
            lift_f32[pl.ds(slot * 2 * tile + place, chans), part] = high[source]
            lift_f32[pl.ds(slot * 2 * tile + tile + place, chans), part] = high[source]
            lift_f32[pl.ds(6 * tile + slot * tile + place, chans), part] = low[source]
    lift_w[...] = lift_f32[...].astype(BF16)
    for layer in range(2):
        for a in range(3):
            for b in range(3):
                tap = transposed(conv_in[layer, 3 * a + b]).astype(BF16)
                for q in range(2):
                    conv_w[
                        layer, pl.ds(((a + q) * 3 + b) * LANES, hidden), pl.ds(q * LANES, hidden)
                    ] = tap
    for q in range(2):
        out_f32[pl.ds(q * chans, chans), pl.ds(q * LANES, hidden)] = out_in[...].astype(F32)
    out_w[...] = out_f32[...].astype(BF16)
    for load in loads[4:]:
        load.wait()

    lane_kind = lane_group < rows // 2

    for u in range(updates):
        receive_all(u)

        def far(slot):
            low_rows = edge_in[u, slot, 2].astype(F32)
            high_rows = edge_in[u, slot, 0].astype(F32)
            kind = jnp.concatenate([lane_kind, lane_kind], axis=0)
            return jnp.where(kind, low_rows, high_rows).astype(BF16)

        sides = [main[u, slot] for slot in range(3)]
        blocks = [[sides[slot][row] for slot in range(3)] for row in range(span)]
        blocks.append([edge_in[u, slot, 1] for slot in range(3)])
        blocks.append([far(slot) for slot in range(3)])
        stacked = jnp.concatenate(
            [jnp.concatenate(block + [part[:tile] for part in block], axis=0) for block in blocks],
            axis=1,
        )
        result = lax.dot_general(
            stacked, lift_w[...], (((0,), (0,)), ((), ())), preferred_element_type=F32
        )
        result = result.astype(BF16).astype(F32)
        own_edge = result[span * cols : (span + 1) * cols]
        far_edge = result[(span + 1) * cols :]
        for row in range(span):
            if row < margin:
                start, edge = group * (rows - margin + row), far_edge
            elif row < margin + rows:
                start, edge = group * (row - margin), own_edge
            else:
                start, edge = group * (row - margin - rows), far_edge
            middle = start + group // 2
            lifted[row, pl.ds(GUARD, cols)] = result[row * cols : (row + 1) * cols]
            lifted[row, pl.ds(0, GUARD)] = edge[middle - GUARD : middle]
            lifted[row, pl.ds(GUARD + cols, GUARD)] = edge[middle : middle + GUARD]
        for row in range(span):
            for b in range(3):
                for frame in range(frames):
                    part = pl.ds(frame * LANES, LANES)
                    lifted_cols[b, row % 2, row // 2, frame] = lifted[
                        row, pl.ds(GUARD - 2 + b, wide), part
                    ].astype(BF16)

        top = jnp.where(l == 0, 0.0, 1.0).astype(F32)
        bottom = jnp.where(l == l_size - 1, 0.0, 1.0).astype(F32)
        pairs = rows // 2 + 1
        for pair in range(pairs):
            window = jnp.concatenate(
                [
                    lifted_cols[b, r % 2, pair + r // 2].reshape(frames * wide, LANES)
                    for r in range(4)
                    for b in range(3)
                ],
                axis=1,
            )
            result = silu(jnp.dot(window, conv_w[0], preferred_element_type=F32))
            for frame in range(frames):
                for q in range(2):
                    value = result[frame * wide : (frame + 1) * wide, q * LANES : (q + 1) * LANES]
                    if pair == 0 and q == 0:
                        value = value * top
                    if pair == pairs - 1 and q == 1:
                        value = value * bottom
                    activated[frame, 2 * pair + q] = value
                    for b in range(3):
                        activated_cols[b, q, pair, frame] = activated[
                            frame, 2 * pair + q, pl.ds(b, cols)
                        ].astype(BF16)

        step = jnp.full((chans, cols), steps_ref[u], F32)
        spread = jnp.sqrt(2.0 * step)
        for pair in range(rows // 2):
            window = jnp.concatenate(
                [
                    activated_cols[b, r % 2, pair + r // 2].reshape(frames * cols, LANES)
                    for r in range(4)
                    for b in range(3)
                ],
                axis=1,
            )
            second = silu(jnp.dot(window, conv_w[1], preferred_element_type=F32))
            base = jnp.concatenate(
                [
                    jnp.concatenate(
                        [
                            lifted[
                                margin + 2 * pair + q, pl.ds(GUARD, cols), pl.ds(frame * LANES, LANES)
                            ]
                            for q in range(2)
                        ],
                        axis=1,
                    )
                    for frame in range(frames)
                ],
                axis=0,
            )
            merged = (base + second).astype(BF16)
            score = lax.dot_general(
                out_w[...], merged, (((1,), (1,)), ((), ())), preferred_element_type=F32
            )
            for q in range(2):
                row = 2 * pair + q
                fresh = []
                for frame in range(frames):
                    where = strided(frame, row)
                    current = state[row, pl.ds(frame * chans, chans)]
                    drift = score[q * chans : (q + 1) * chans, frame * cols : (frame + 1) * cols]
                    pull = obs_weight[where, :] * (observed[where, :] - current)
                    value = current + step * (drift + pull) + spread * noise[u, where, :]
                    fresh.append(value)
                    if u == updates - 1:
                        result_ref[where, :] = value
                if u < updates - 1:
                    keep(u + 1, row, jnp.concatenate(fresh, axis=0))
            if u < updates - 1:
                send_chunk(u + 1, pair)
        if u < updates - 1:
            send_edges(u + 1)

    for u in range(updates):
        for dt, dl, do in around:

            @pl.when(exists(dt, dl))
            def _():
                for chunk in chunks_of(u, dl, do):
                    message(u, dt, dl, do, chunk).wait_send()


def per_device(
    prior_state, observed, obs_weight, noise_field, step_sizes, lift_weight, conv_weights, out_weight
):
    frames, chans, rows, cols = prior_state.shape
    hidden, depth = lift_weight.shape
    updates = noise_field.shape[0]
    margin = 2
    tile = frames * chans
    span = rows + 2 * margin
    wide = cols + 2 * GUARD
    flat = (tile * rows, cols)
    dims = (frames, chans, rows, cols, hidden, updates, margin)
    vmem = pltpu.VMEM
    result = pl.pallas_call(
        functools.partial(kernel, dims),
        out_shape=jax.ShapeDtypeStruct(flat, F32),
        in_specs=[pl.BlockSpec(memory_space=pltpu.SMEM)] + [pl.BlockSpec(memory_space=pl.ANY)] * 7,
        out_specs=pl.BlockSpec(memory_space=pltpu.VMEM),
        scratch_shapes=[
            vmem(flat, F32),
            vmem(flat, F32),
            vmem(flat, F32),
            vmem((updates, *flat), F32),
            vmem((depth, hidden), F32),
            vmem(conv_weights.shape, BF16),
            vmem(out_weight.shape, BF16),
            pltpu.SemaphoreType.DMA((7,)),
            pltpu.SemaphoreType.DMA((updates, 18 * (rows // margin))),
            pltpu.SemaphoreType.DMA((updates, 18 * (rows // margin))),
            vmem((rows, tile, cols), F32),
            vmem((updates, 3, span, 2 * tile, cols), BF16),
            vmem((updates, 2 * tile, cols), BF16),
            vmem((updates, 3, 3, 2 * tile, cols), BF16),
            vmem((9 * tile, frames * LANES), F32),
            vmem((9 * tile, frames * LANES), BF16),
            vmem((2, 12 * LANES, 2 * LANES), BF16),
            vmem((2 * chans, 2 * LANES), F32),
            vmem((2 * chans, 2 * LANES), BF16),
            vmem((span, wide + GUARD, frames * LANES), F32),
            vmem((3, 2, span // 2, frames, wide, LANES), BF16),
            vmem((frames, rows + 2, wide, LANES), F32),
            vmem((3, 2, rows // 2 + 1, frames, cols, LANES), BF16),
        ],
        compiler_params=pltpu.CompilerParams(
            collective_id=0, has_side_effects=True, vmem_limit_bytes=60 * 1024 * 1024
        ),
        cost_estimate=pl.CostEstimate(
            flops=4 * updates * tile * rows * cols * hidden * 9 * hidden // chans,
            bytes_accessed=1 << 20,
            transcendentals=0,
        ),
    )(
        step_sizes,
        prior_state.reshape(flat),
        observed.reshape(flat),
        obs_weight.reshape(flat),
        noise_field.reshape(updates, *flat),
        lift_weight.T,
        conv_weights,
        out_weight,
    )
    return result.reshape(prior_state.shape)


def solution(mesh):
    placed = (
        P(("groups", "tm"), None, "lat", "lon"),
        P(("groups", "tm"), None, "lat", "lon"),
        P(("groups", "tm"), None, "lat", "lon"),
        P(None, ("groups", "tm"), None, "lat", "lon"),
        P(),
        P(),
        P(),
        P(),
    )
    return jax.shard_map(
        per_device,
        mesh=mesh,
        in_specs=placed,
        out_specs=P(("groups", "tm"), None, "lat", "lon"),
        check_vma=False,
    )
```

time: 28.7 us -> 27.7 us (0.965)
  local copies, waits for them, and re-layouts: 5.08 us -> 1.47 us
  Pallas kernels: 23.3 us -> 26 us
    unnamed x16 -> x1, local copies, waits for them, and re-layouts: 5.08 us -> 1.47 us
    pallas_call x1, Pallas kernels: 23.3 us -> 26 us  [per_device(): pl.pallas_call(functools.partial(kernel, dims), out_shape=jax.ShapeDtypeS...]
where the time goes in v2:
time: 27.7 us; the launch traced here: 27.5 us
  Pallas kernels  26 us (94%)
  local copies, waits for them, and re-layouts  1.47 us (5%)
    pallas_call x1, Pallas kernels, per_device(): pl.pallas_call(functools.partial(kernel, dims), out_shape=jax.ShapeDtypeS...  26 us
    unnamed x1, local copies, waits for them, and re-layouts  1.47 us

profile of v2, /device:TPU:0, one launch (start us, length us, event | category | flops | bytes accessed | tf_op | source)
XLA Modules:
  0.0 27.5 jit_solution(15788932519793930853)
XLA Ops:
  0.0 26.0 %shard_map.82 = f32[128,128]{1,0:T(8,128)} custom-call(f32[2]{0:T(128)} %steps_ref.1, f32[128,128]{1,0:T(8,128)} %bitcast.8, f32[128,128]{1,0:T(8,128)} %bitcast.9, f32[128,128]{1,0:T(8,128)} %bitcast.10, f32[2,128,128]{2,1,0:T(8,128)} %bitcast.7, f32[40,96]{1,0:T(8,128)} %bitcast.11, bf16[2,9,96,96]{3,2,1,0:T(8,128)(2,1)} %conv_hbm.1, ...), custom_call_target="tpu_custom_call" | custom-call | flops 1358954496 | bytes 1048576 | tf_op jit(solution)/shard_map/pallas_call | solution.py:382
  26.0 1.5 %copy.10 = f32[2,8,8,128]{3,2,1,0:T(8,128)} copy(f32[2,8,8,128]{3,2,1,0:T(8,128)} %bitcast.6) | data formatting | bytes 131072

commit v3 on v2

--- a/solution.py
+++ b/solution.py
@@ -118,7 +118,7 @@
 
     def message(u, dt, dl, do, chunk=0):
         slot, kind = 1 - dt, 1 - dl
-        first, count = (margin * chunk, margin) if u else (0, rows)
+        first, count = margin * chunk, margin
         if do:
             source, place = edge_out.at[u], edge_in.at[u, slot, kind]
         elif dl == 0:
@@ -151,8 +151,8 @@
         def _():
             message(u, dt, dl, do, chunk).start()
 
-    def chunks_of(u, dl, do):
-        return range(rows // margin) if u and dl == 0 and not do else range(1)
+    def chunks_of(dl, do):
+        return range(rows // margin) if dl == 0 and not do else range(1)
 
     def keep(u, row, value):
         state[row] = value
@@ -161,10 +161,14 @@
     def send_chunk(u, chunk):
         for dt in (-1, 1):
             send(u, dt, 0, 0, chunk)
-        if chunk == 0:
+
+        @pl.when(chunk == 0)
+        def _():
             for dt in (-1, 0, 1):
                 send(u, dt, -1, 0)
-        if chunk == rows // margin - 1:
+
+        @pl.when(chunk == rows // margin - 1)
+        def _():
             for dt in (-1, 0, 1):
                 send(u, dt, 1, 0)
 
@@ -183,7 +187,7 @@
 
             @pl.when(exists(-dt, -dl))
             def _():
-                for chunk in chunks_of(u, dl, do):
+                for chunk in chunks_of(dl, do):
                     message(u, dt, dl, do, chunk).wait_recv()
 
     def strided(frame, row):
@@ -197,11 +201,12 @@
             jnp.concatenate([prior[strided(frame, row), :] for frame in range(frames)], axis=0),
         )
     pl.semaphore_wait(barrier, t_count * l_count * 2 - 1)
-    for dt in (-1, 1):
-        send(0, dt, 0, 0)
-    for dt in (-1, 0, 1):
-        for dl in (-1, 1):
-            send(0, dt, dl, 0)
+
+    def send_first(chunk, carry):
+        send_chunk(0, chunk)
+        return carry
+
+    lax.fori_loop(0, rows // margin, send_first, 0)
     send_edges(0)
 
     lift_f32[...] = jnp.zeros_like(lift_f32)
@@ -239,7 +244,7 @@
 
     lane_kind = lane_group < rows // 2
 
-    for u in range(updates):
+    def update(u, carry):
         receive_all(u)
 
         def far(slot):
@@ -284,7 +289,10 @@
         top = jnp.where(l == 0, 0.0, 1.0).astype(F32)
         bottom = jnp.where(l == l_size - 1, 0.0, 1.0).astype(F32)
         pairs = rows // 2 + 1
-        for pair in range(pairs):
+
+        def first_conv(pair, carry):
+            above = jnp.where(pair == 0, top, 1.0)
+            below = jnp.where(pair == pairs - 1, bottom, 1.0)
             window = jnp.concatenate(
                 [
                     lifted_cols[b, r % 2, pair + r // 2].reshape(frames * wide, LANES)
@@ -297,19 +305,20 @@
             for frame in range(frames):
                 for q in range(2):
                     value = result[frame * wide : (frame + 1) * wide, q * LANES : (q + 1) * LANES]
-                    if pair == 0 and q == 0:
-                        value = value * top
-                    if pair == pairs - 1 and q == 1:
-                        value = value * bottom
+                    value = value * (below if q else above)
                     activated[frame, 2 * pair + q] = value
                     for b in range(3):
                         activated_cols[b, q, pair, frame] = activated[
                             frame, 2 * pair + q, pl.ds(b, cols)
                         ].astype(BF16)
+            return carry
+
+        lax.fori_loop(0, pairs, first_conv, 0)
 
         step = jnp.full((chans, cols), steps_ref[u], F32)
         spread = jnp.sqrt(2.0 * step)
-        for pair in range(rows // 2):
+
+        def second_conv(pair, carry):
             window = jnp.concatenate(
                 [
                     activated_cols[b, r % 2, pair + r // 2].reshape(frames * cols, LANES)
@@ -348,21 +357,31 @@
                     pull = obs_weight[where, :] * (observed[where, :] - current)
                     value = current + step * (drift + pull) + spread * noise[u, where, :]
                     fresh.append(value)
-                    if u == updates - 1:
-                        result_ref[where, :] = value
-                if u < updates - 1:
-                    keep(u + 1, row, jnp.concatenate(fresh, axis=0))
-            if u < updates - 1:
+                    result_ref[where, :] = value
+                keep(u + 1, row, jnp.concatenate(fresh, axis=0))
+
+            @pl.when(u < updates - 1)
+            def _():
                 send_chunk(u + 1, pair)
-        if u < updates - 1:
+
+            return carry
+
+        lax.fori_loop(0, rows // 2, second_conv, 0)
+
+        @pl.when(u < updates - 1)
+        def _():
             send_edges(u + 1)
+
+        return carry
+
+    lax.fori_loop(0, updates, update, 0)
 
     for u in range(updates):
         for dt, dl, do in around:
 
             @pl.when(exists(dt, dl))
             def _():
-                for chunk in chunks_of(u, dl, do):
+                for chunk in chunks_of(dl, do):
                     message(u, dt, dl, do, chunk).wait_send()
 
 
@@ -396,7 +415,7 @@
             pltpu.SemaphoreType.DMA((updates, 18 * (rows // margin))),
             pltpu.SemaphoreType.DMA((updates, 18 * (rows // margin))),
             vmem((rows, tile, cols), F32),
-            vmem((updates, 3, span, 2 * tile, cols), BF16),
+            vmem((updates + 1, 3, span, 2 * tile, cols), BF16),
             vmem((updates, 2 * tile, cols), BF16),
             vmem((updates, 3, 3, 2 * tile, cols), BF16),
             vmem((9 * tile, frames * LANES), F32),

time: 27.7 us -> 29 us (1.047)
  Pallas kernels: 26 us -> 27.4 us
    pallas_call x1, Pallas kernels: 26 us -> 27.4 us  [per_device(): pl.pallas_call(functools.partial(kernel, dims), out_shape=jax.ShapeDtypeS...]
where the time goes in v3:
time: 29 us; the launch traced here: 28.8 us
  Pallas kernels  27.4 us (94%)
  local copies, waits for them, and re-layouts  1.47 us (5%)
    pallas_call x1, Pallas kernels, per_device(): pl.pallas_call(functools.partial(kernel, dims), out_shape=jax.ShapeDtypeS...  27.4 us
    unnamed x1, local copies, waits for them, and re-layouts  1.47 us

profile of v3, /device:TPU:0, one launch (start us, length us, event | category | flops | bytes accessed | tf_op | source)
XLA Modules:
  0.0 28.8 jit_solution(3361176505572821994)
XLA Ops:
  0.0 27.4 %shard_map.82 = f32[128,128]{1,0:T(8,128)} custom-call(f32[2]{0:T(128)} %steps_ref.1, f32[128,128]{1,0:T(8,128)} %bitcast.8, f32[128,128]{1,0:T(8,128)} %bitcast.9, f32[128,128]{1,0:T(8,128)} %bitcast.10, f32[2,128,128]{2,1,0:T(8,128)} %bitcast.7, f32[40,96]{1,0:T(8,128)} %bitcast.11, bf16[2,9,96,96]{3,2,1,0:T(8,128)(2,1)} %conv_hbm.1, ...), custom_call_target="tpu_custom_call" | custom-call | flops 1358954496 | bytes 1048576 | tf_op jit(solution)/shard_map/pallas_call | solution.py:401
  27.4 1.5 %copy.10 = f32[2,8,8,128]{3,2,1,0:T(8,128)} copy(f32[2,8,8,128]{3,2,1,0:T(8,128)} %bitcast.6) | data formatting | bytes 131072

commit v4 on v3

v4 whole, which is shorter than its diff:
```python
import functools

import jax
import jax.numpy as jnp
from jax import lax
from jax.experimental import pallas as pl
from jax.experimental.pallas import tpu as pltpu
from jax.sharding import PartitionSpec as P

F32 = jnp.float32
BF16 = jnp.bfloat16
LANES = 128


def silu(value):
    half = 0.5 * value
    return half + half * jnp.tanh(half)


def kernel(
    dims,
    steps_ref,
    prior_hbm,
    observed_hbm,
    obs_weight_hbm,
    noise_hbm,
    lift_hbm,
    conv_hbm,
    out_weight_hbm,
    result_ref,
    prior,
    observed,
    obs_weight,
    noise,
    lift_in,
    conv_in,
    out_in,
    load_sem,
    send_sem,
    recv_sem,
    state,
    main,
    edge_out,
    edge_in,
    lift_f32,
    lift_w,
    conv_w,
    out_w,
    lifted_cols,
    activated_cols,
):
    frames, chans, rows, cols, hidden, updates, margin = dims
    tile = frames * chans
    group = cols // rows
    span = rows + 2 * margin
    t, t_size = lax.axis_index("tm"), lax.axis_size("tm")
    l, l_size = lax.axis_index("lat"), lax.axis_size("lat")
    other = lax.rem(lax.axis_index("lon") + 1, lax.axis_size("lon"))

    loads = [
        pltpu.make_async_copy(source, target, load_sem.at[index])
        for index, (source, target) in enumerate(
            (
                (prior_hbm, prior),
                (conv_hbm, conv_in),
                (lift_hbm, lift_in),
                (out_weight_hbm, out_in),
                (observed_hbm, observed),
                (obs_weight_hbm, obs_weight),
                (noise_hbm, noise),
            )
        )
    ]
    for load in loads:
        load.start()

    main[...] = jnp.zeros_like(main)
    edge_in[...] = jnp.zeros_like(edge_in)

    around = [
        (dt, dl, do)
        for dt in (-1, 0, 1)
        for dl in (-1, 0, 1)
        for do in (0, 1)
        if (dt, dl, do) != (0, 0, 0)
    ]

    def exists(dt, dl):
        return (t + dt >= 0) & (t + dt < t_size) & (l + dl >= 0) & (l + dl < l_size)

    def target(dt, dl, do):
        own = lax.axis_index("lon")
        return {"tm": t + dt, "lat": l + dl, "lon": other if do else own}

    barrier = pltpu.get_barrier_semaphore()
    for dt, dl, do in around:

        @pl.when(exists(dt, dl))
        def _():
            pl.semaphore_signal(
                barrier, inc=1, device_id=target(dt, dl, do), device_id_type=pl.DeviceIdType.MESH
            )

    def one(flag):
        return flag.astype(jnp.int32)

    t_count = 1 + one(t > 0) + one(t < t_size - 1)
    l_count = 1 + one(l > 0) + one(l < l_size - 1)

    def message(u, dt, dl, do, chunk=0):
        slot, kind = 1 - dt, 1 - dl
        first, count = margin * chunk, margin
        if do:
            source, place = edge_out.at[u], edge_in.at[u, slot, kind, do - 1]
        elif dl == 0:
            source = main.at[u, 1, pl.ds(margin + first, count)]
            place = main.at[u, slot, pl.ds(margin + first, count)]
        elif dl == 1:
            source = main.at[u, 1, pl.ds(rows, margin)]
            place = main.at[u, slot, pl.ds(0, margin)]
        else:
            source = main.at[u, 1, pl.ds(margin, margin)]
            place = main.at[u, slot, pl.ds(margin + rows, margin)]
        where = ((slot * 3 + kind) * 3 + do) * (rows // margin) + chunk
        return pltpu.make_async_remote_copy(
            src_ref=source,
            dst_ref=place,
            send_sem=send_sem.at[u, where],
            recv_sem=recv_sem.at[u, where],
            device_id=target(dt, dl, do == 1),
            device_id_type=pl.DeviceIdType.MESH,
        )

    lane = lax.broadcasted_iota(jnp.int32, (tile, cols), 1)
    lane_group = lane // group
    lane_half = lane % group < group // 2

    def halves(value):
        high = value.astype(BF16)
        return jnp.concatenate([high, (value - high.astype(F32)).astype(BF16)], axis=0)

    def send(u, dt, dl, do, chunk=0):
        @pl.when(exists(dt, dl))
        def _():
            message(u, dt, dl, do, chunk).start()

    def chunks_of(dl, do):
        return range(rows // margin) if dl == 0 and not do else range(1)

    def keep(u, row, value):
        state[row] = value
        main[u, 1, margin + row] = halves(value)

    def send_chunk(u, chunk):
        for dt in (-1, 1):
            send(u, dt, 0, 0, chunk)

        if chunk == 0:
            for dt in (-1, 0, 1):
                send(u, dt, -1, 0)
        if chunk == rows // margin - 1:
            for dt in (-1, 0, 1):
                send(u, dt, 1, 0)

    def send_edges(u):
        edge = jnp.zeros((tile, cols), F32)
        for row in range(rows):
            value = state[row]
            first = pltpu.roll(value, (group * row + group // 4) % cols, 1)
            last = pltpu.roll(value, (group * row + 3 * group // 4) % cols, 1)
            edge = jnp.where(lane_group == row, jnp.where(lane_half, first, last), edge)
        edge_out[u] = halves(edge)
        for dt in (-1, 0, 1):
            for dl in (-1, 0, 1):
                send(u, dt, dl, 1)
                if dt or dl:
                    send(u, dt, dl, 2)

    sent = around + [(dt, dl, 2) for dt, dl, do in around if not do]

    def receive_all(u):
        for dt, dl, do in sent:

            @pl.when(exists(-dt, -dl))
            def _():
                for chunk in chunks_of(dl, do):
                    message(u, dt, dl, do, chunk).wait_recv()

    def strided(frame, row):
        return pl.ds(frame * chans * rows + row, chans, stride=rows)

    loads[0].wait()
    for row in range(rows):
        keep(
            0,
            row,
            jnp.concatenate([prior[strided(frame, row), :] for frame in range(frames)], axis=0),
        )
    pl.semaphore_wait(barrier, t_count * l_count * 2 - 1)

    for chunk in range(rows // margin):
        send_chunk(0, chunk)
    send_edges(0)

    lift_f32[...] = jnp.zeros_like(lift_f32)
    for load in loads[1:4]:
        load.wait()
    depth = lift_in.shape[0]
    turned = lift_in[...]
    high = turned.astype(BF16).astype(F32)
    low = turned - high
    for frame in range(frames):
        part = pl.ds(frame * LANES, hidden)
        for item in range(depth // chans):
            source = slice(item * chans, (item + 1) * chans)
            slot, place = divmod((item + frame) * chans, tile)
            lift_f32[pl.ds(slot * 2 * tile + place, chans), part] = high[source]
            lift_f32[pl.ds(slot * 2 * tile + tile + place, chans), part] = high[source]
            lift_f32[pl.ds(6 * tile + slot * tile + place, chans), part] = low[source]
    turned = jnp.transpose(lift_f32[...])
    for frame in range(frames):
        lift_w[pl.ds(frame * hidden, hidden)] = turned[
            frame * LANES : frame * LANES + hidden
        ].astype(BF16)
    for layer in range(2):
        taps = [conv_in[layer, tap] for tap in range(9)]
        empty = [jnp.zeros((hidden, hidden), BF16)] * 3
        conv_w[layer, pl.ds(0, hidden)] = jnp.concatenate(taps + empty, axis=1)
        conv_w[layer, pl.ds(hidden, hidden)] = jnp.concatenate(empty + taps, axis=1)
    project = out_in[...].astype(F32)
    blank = jnp.zeros_like(project)
    out_w[...] = jnp.concatenate(
        [jnp.concatenate([project, blank], axis=1), jnp.concatenate([blank, project], axis=1)],
        axis=0,
    ).astype(BF16)
    for load in loads[4:]:
        load.wait()

    lane_tall = lax.broadcasted_iota(jnp.int32, (2 * tile, cols), 1)
    own_lanes = (lane_tall % group >= group // 4) & (lane_tall % group < 3 * group // 4)
    low_lanes = lane_tall < cols // 2
    edge_lane = lax.broadcasted_iota(jnp.int32, (hidden, 2 * cols), 1)

    def shifted(value, edge, row, b):
        first = (group * row + group // 4 - 1) % (2 * cols)
        last = (group * row + 3 * group // 4) % (2 * cols)
        if b == 0:
            return jnp.concatenate([edge[:, first : first + 1], value[:, : cols - 1]], axis=1)
        if b == 2:
            return jnp.concatenate([value[:, 1:], edge[:, last : last + 1]], axis=1)
        return value

    def update(u, carry):
        receive_all(u)

        def rim(slot, kind):
            same = edge_out[u] if (slot, kind) == (1, 1) else edge_in[u, slot, kind, 1]
            return jnp.where(own_lanes, same.astype(F32), edge_in[u, slot, kind, 0].astype(F32))

        blocks = [[main[u, slot, row] for slot in range(3)] for row in range(span)]
        blocks.append([rim(slot, 1).astype(BF16) for slot in range(3)])
        blocks.append(
            [jnp.where(low_lanes, rim(slot, 2), rim(slot, 0)).astype(BF16) for slot in range(3)]
        )
        stacked = jnp.concatenate(
            [jnp.concatenate(block + [part[:tile] for part in block], axis=0) for block in blocks],
            axis=1,
        )
        result = jnp.dot(lift_w[...], stacked, preferred_element_type=F32).astype(BF16)
        edges = []
        for frame in range(frames):
            whole = result[frame * hidden : (frame + 1) * hidden]
            part = pl.ds(frame * cols, cols)
            edge = whole[:, span * cols :]
            edges.append(edge)
            for row in range(span):
                value = whole[:, row * cols : (row + 1) * cols]
                for b in range(3):
                    lifted_cols[b, row, :, part] = shifted(value, edge, row - margin, b)

        top = jnp.where(l == 0, 0.0, 1.0).astype(F32)
        bottom = jnp.where(l == l_size - 1, 0.0, 1.0).astype(F32)
        pairs = rows // 2 + 1
        for frame in range(frames):
            turns = []
            for a in range(-1, 2):
                for b in range(-1, 2):
                    turn = (group * a + b) % (2 * cols)
                    edge = edges[frame]
                    if turn:
                        edge = jnp.concatenate([edge[:, turn:], edge[:, :turn]], axis=1)
                    turns.append(edge)
            value = silu(
                jnp.dot(
                    conv_w[0, pl.ds(0, hidden), pl.ds(0, 9 * hidden)],
                    jnp.concatenate(turns, axis=0),
                    preferred_element_type=F32,
                )
            )
            value = jnp.where(edge_lane >= 2 * cols - group, value * top, value)
            after = (edge_lane >= cols) & (edge_lane < cols + group)
            edges[frame] = jnp.where(after, value * bottom, value).astype(BF16)

        for pair in range(pairs):
            window = jnp.concatenate(
                [lifted_cols[b, 2 * pair + r] for r in range(4) for b in range(3)], axis=0
            )
            result = silu(jnp.dot(conv_w[0], window, preferred_element_type=F32))
            for q in range(2):
                value = result[q * hidden : (q + 1) * hidden]
                if pair == 0 and q == 0:
                    value = value * top
                if pair == pairs - 1 and q == 1:
                    value = value * bottom
                value = value.astype(BF16)
                row = 2 * pair + q
                for frame in range(frames):
                    own = value[:, frame * cols : (frame + 1) * cols]
                    for b in range(3):
                        activated_cols[b, row, :, pl.ds(frame * cols, cols)] = shifted(
                            own, edges[frame], row - 1, b
                        )

        step = jnp.full((chans, cols), steps_ref[u], F32)
        spread = jnp.sqrt(2.0 * step)

        for pair in range(rows // 2):
            window = jnp.concatenate(
                [activated_cols[b, 2 * pair + r] for r in range(4) for b in range(3)], axis=0
            )
            second = silu(jnp.dot(conv_w[1], window, preferred_element_type=F32))
            base = jnp.concatenate(
                [lifted_cols[1, margin + 2 * pair + q] for q in range(2)], axis=0
            )
            merged = (base.astype(F32) + second).astype(BF16)
            score = jnp.dot(out_w[...], merged, preferred_element_type=F32)
            for q in range(2):
                row = 2 * pair + q
                fresh = []
                for frame in range(frames):
                    where = strided(frame, row)
                    current = state[row, pl.ds(frame * chans, chans)]
                    drift = score[q * chans : (q + 1) * chans, frame * cols : (frame + 1) * cols]
                    pull = obs_weight[where, :] * (observed[where, :] - current)
                    value = current + step * (drift + pull) + spread * noise[u, where, :]
                    fresh.append(value)
                    result_ref[where, :] = value
                keep(u + 1, row, jnp.concatenate(fresh, axis=0))

            @pl.when(u < updates - 1)
            def _():
                send_chunk(u + 1, pair)

        @pl.when(u < updates - 1)
        def _():
            send_edges(u + 1)

        return carry

    lax.fori_loop(0, updates, update, 0)

    for u in range(updates):
        for dt, dl, do in sent:

            @pl.when(exists(dt, dl))
            def _():
                for chunk in chunks_of(dl, do):
                    message(u, dt, dl, do, chunk).wait_send()


def per_device(
    prior_state, observed, obs_weight, noise_field, step_sizes, lift_weight, conv_weights, out_weight
):
    frames, chans, rows, cols = prior_state.shape
    hidden, depth = lift_weight.shape
    updates = noise_field.shape[0]
    margin = 2
    tile = frames * chans
    span = rows + 2 * margin
    flat = (tile * rows, cols)
    dims = (frames, chans, rows, cols, hidden, updates, margin)
    vmem = pltpu.VMEM
    result = pl.pallas_call(
        functools.partial(kernel, dims),
        out_shape=jax.ShapeDtypeStruct(flat, F32),
        in_specs=[pl.BlockSpec(memory_space=pltpu.SMEM)] + [pl.BlockSpec(memory_space=pl.ANY)] * 7,
        out_specs=pl.BlockSpec(memory_space=pltpu.VMEM),
        scratch_shapes=[
            vmem(flat, F32),
            vmem(flat, F32),
            vmem(flat, F32),
            vmem((updates, *flat), F32),
            vmem((depth, hidden), F32),
            vmem(conv_weights.shape, BF16),
            vmem(out_weight.shape, BF16),
            pltpu.SemaphoreType.DMA((7,)),
            pltpu.SemaphoreType.DMA((updates, 27 * (rows // margin))),
            pltpu.SemaphoreType.DMA((updates, 27 * (rows // margin))),
            vmem((rows, tile, cols), F32),
            vmem((updates + 1, 3, span, 2 * tile, cols), BF16),
            vmem((updates, 2 * tile, cols), BF16),
            vmem((updates, 3, 3, 2, 2 * tile, cols), BF16),
            vmem((9 * tile, frames * LANES), F32),
            vmem((frames * hidden, 9 * tile), BF16),
            vmem((2, 2 * hidden, 12 * hidden), BF16),
            vmem((2 * chans, 2 * hidden), BF16),
            vmem((3, span, hidden, frames * cols), BF16),
            vmem((3, rows + 2, hidden, frames * cols), BF16),
        ],
        compiler_params=pltpu.CompilerParams(
            collective_id=0, has_side_effects=True, vmem_limit_bytes=60 * 1024 * 1024
        ),
        cost_estimate=pl.CostEstimate(
            flops=4 * updates * tile * rows * cols * hidden * 9 * hidden // chans,
            bytes_accessed=1 << 20,
            transcendentals=0,
        ),
    )(
        step_sizes,
        prior_state.reshape(flat),
        observed.reshape(flat),
        obs_weight.reshape(flat),
        noise_field.reshape(updates, *flat),
        lift_weight.T,
        conv_weights,
        out_weight,
    )
    return result.reshape(prior_state.shape)


def solution(mesh):
    placed = (
        P(("groups", "tm"), None, "lat", "lon"),
        P(("groups", "tm"), None, "lat", "lon"),
        P(("groups", "tm"), None, "lat", "lon"),
        P(None, ("groups", "tm"), None, "lat", "lon"),
        P(),
        P(),
        P(),
        P(),
    )
    return jax.shard_map(
        per_device,
        mesh=mesh,
        in_specs=placed,
        out_specs=P(("groups", "tm"), None, "lat", "lon"),
        check_vma=False,
    )
```

time: 29 us -> 27.6 us (0.952)
  Pallas kernels: 27.4 us -> 26 us
    pallas_call x1, Pallas kernels: 27.4 us -> 26 us  [per_device(): pl.pallas_call(functools.partial(kernel, dims), out_shape=jax.ShapeDtypeS...]
where the time goes in v4:
time: 27.6 us; the launch traced here: 27.5 us
  Pallas kernels  26 us (94%)
  local copies, waits for them, and re-layouts  1.47 us (5%)
    pallas_call x1, Pallas kernels, per_device(): pl.pallas_call(functools.partial(kernel, dims), out_shape=jax.ShapeDtypeS...  26 us
    unnamed x1, local copies, waits for them, and re-layouts  1.47 us

profile of v4, /device:TPU:0, one launch (start us, length us, event | category | flops | bytes accessed | tf_op | source)
XLA Modules:
  0.0 27.5 jit_solution(6034734020494242016)
XLA Ops:
  0.0 26.0 %shard_map.82 = f32[128,128]{1,0:T(8,128)} custom-call(f32[2]{0:T(128)} %steps_ref.1, f32[128,128]{1,0:T(8,128)} %bitcast.8, f32[128,128]{1,0:T(8,128)} %bitcast.9, f32[128,128]{1,0:T(8,128)} %bitcast.10, f32[2,128,128]{2,1,0:T(8,128)} %bitcast.7, f32[40,96]{1,0:T(8,128)} %bitcast.11, bf16[2,9,96,96]{3,2,1,0:T(8,128)(2,1)} %conv_hbm.1, ...), custom_call_target="tpu_custom_call" | custom-call | flops 1358954496 | bytes 1048576 | tf_op jit(solution)/shard_map/pallas_call | solution.py:383
  26.0 1.5 %copy.10 = f32[2,8,8,128]{3,2,1,0:T(8,128)} copy(f32[2,8,8,128]{3,2,1,0:T(8,128)} %bitcast.6) | data formatting | bytes 131072

commit v5 on v4

--- a/solution.py
+++ b/solution.py
@@ -40,7 +40,6 @@
     recv_sem,
     state,
     main,
-    edge_out,
     edge_in,
     lift_f32,
     lift_w,
@@ -74,8 +73,30 @@
     for load in loads:
         load.start()
 
-    main[...] = jnp.zeros_like(main)
-    edge_in[...] = jnp.zeros_like(edge_in)
+    head = margin + 1
+    own_start = head + 1
+    own_edge = own_start + rows
+    tail = own_edge + 1
+
+    def cleared(ref):
+        ref[...] = jnp.zeros(ref.shape, ref.dtype)
+
+    for u in range(updates):
+        for slot, absent in ((0, t == 0), (2, t == t_size - 1)):
+
+            @pl.when(absent)
+            def _():
+                cleared(main.at[u, slot])
+                cleared(edge_in.at[u, slot])
+
+        for kind, first, absent in ((0, 0, l == 0), (2, tail, l == l_size - 1)):
+
+            @pl.when(absent)
+            def _():
+                for slot in range(3):
+                    cleared(main.at[u, slot, pl.ds(first, head)])
+                    cleared(edge_in.at[u, slot, kind])
+
 
     around = [
         (dt, dl, do)
@@ -109,25 +130,25 @@
 
     def message(u, dt, dl, do, chunk=0):
         slot, kind = 1 - dt, 1 - dl
-        first, count = margin * chunk, margin
         if do:
-            source, place = edge_out.at[u], edge_in.at[u, slot, kind, do - 1]
-        elif dl == 0:
-            source = main.at[u, 1, pl.ds(margin + first, count)]
-            place = main.at[u, slot, pl.ds(margin + first, count)]
-        elif dl == 1:
-            source = main.at[u, 1, pl.ds(rows, margin)]
-            place = main.at[u, slot, pl.ds(0, margin)]
+            source, place = main.at[u, 1, own_edge], edge_in.at[u, slot, kind]
         else:
-            source = main.at[u, 1, pl.ds(margin, margin)]
-            place = main.at[u, slot, pl.ds(margin + rows, margin)]
-        where = ((slot * 3 + kind) * 3 + do) * (rows // margin) + chunk
+            if dl == 1 or (dl == 0 and chunk == 1):
+                first, count = own_edge - margin, head
+            elif dl == 0:
+                first, count = own_start, rows - margin
+            else:
+                first, count = head, head
+            landing = {1: 0, 0: first, -1: tail}[dl]
+            source = main.at[u, 1, pl.ds(first, count)]
+            place = main.at[u, slot, pl.ds(landing, count)]
+        where = ((slot * 3 + kind) * 2 + do) * 2 + chunk
         return pltpu.make_async_remote_copy(
             src_ref=source,
             dst_ref=place,
             send_sem=send_sem.at[u, where],
             recv_sem=recv_sem.at[u, where],
-            device_id=target(dt, dl, do == 1),
+            device_id=target(dt, dl, do),
             device_id_type=pl.DeviceIdType.MESH,
         )
 
@@ -145,22 +166,15 @@
             message(u, dt, dl, do, chunk).start()
 
     def chunks_of(dl, do):
-        return range(rows // margin) if dl == 0 and not do else range(1)
+        return range(2) if dl == 0 and not do else range(1)
 
     def keep(u, row, value):
         state[row] = value
-        main[u, 1, margin + row] = halves(value)
-
-    def send_chunk(u, chunk):
+        main[u, 1, own_start + row] = halves(value)
+
+    def send_early(u):
         for dt in (-1, 1):
-            send(u, dt, 0, 0, chunk)
-
-        if chunk == 0:
-            for dt in (-1, 0, 1):
-                send(u, dt, -1, 0)
-        if chunk == rows // margin - 1:
-            for dt in (-1, 0, 1):
-                send(u, dt, 1, 0)
+            send(u, dt, 0, 0, 0)
 
     def send_edges(u):
         edge = jnp.zeros((tile, cols), F32)
@@ -169,17 +183,18 @@
             first = pltpu.roll(value, (group * row + group // 4) % cols, 1)
             last = pltpu.roll(value, (group * row + 3 * group // 4) % cols, 1)
             edge = jnp.where(lane_group == row, jnp.where(lane_half, first, last), edge)
-        edge_out[u] = halves(edge)
-        for dt in (-1, 0, 1):
-            for dl in (-1, 0, 1):
+        main[u, 1, head] = halves(edge)
+        main[u, 1, own_edge] = halves(edge)
+        for dt in (-1, 1):
+            send(u, dt, 0, 0, 1)
+        for dt in (-1, 1, 0):
+            for dl in (-1, 1):
+                send(u, dt, dl, 0)
+            for dl in (-1, 1, 0):
                 send(u, dt, dl, 1)
-                if dt or dl:
-                    send(u, dt, dl, 2)
-
-    sent = around + [(dt, dl, 2) for dt, dl, do in around if not do]
 
     def receive_all(u):
-        for dt, dl, do in sent:
+        for dt, dl, do in around:
 
             @pl.when(exists(-dt, -dl))
             def _():
@@ -198,8 +213,7 @@
         )
     pl.semaphore_wait(barrier, t_count * l_count * 2 - 1)
 
-    for chunk in range(rows // margin):
-        send_chunk(0, chunk)
+    send_early(0)
     send_edges(0)
 
     lift_f32[...] = jnp.zeros_like(lift_f32)
@@ -254,10 +268,14 @@
         receive_all(u)
 
         def rim(slot, kind):
-            same = edge_out[u] if (slot, kind) == (1, 1) else edge_in[u, slot, kind, 1]
-            return jnp.where(own_lanes, same.astype(F32), edge_in[u, slot, kind, 0].astype(F32))
-
-        blocks = [[main[u, slot, row] for slot in range(3)] for row in range(span)]
+            same = main[u, slot, (margin, own_edge, tail)[kind]]
+            return jnp.where(own_lanes, same.astype(F32), edge_in[u, slot, kind].astype(F32))
+
+        tiles = [
+            row + (2 if row >= margin else 0) + (2 if row >= margin + rows else 0)
+            for row in range(span)
+        ]
+        blocks = [[main[u, slot, place] for slot in range(3)] for place in tiles]
         blocks.append([rim(slot, 1).astype(BF16) for slot in range(3)])
         blocks.append(
             [jnp.where(low_lanes, rim(slot, 2), rim(slot, 0)).astype(BF16) for slot in range(3)]
@@ -334,6 +352,7 @@
             )
             merged = (base.astype(F32) + second).astype(BF16)
             score = jnp.dot(out_w[...], merged, preferred_element_type=F32)
+            fresh_rows = []
             for q in range(2):
                 row = 2 * pair + q
                 fresh = []
@@ -345,11 +364,14 @@
                     value = current + step * (drift + pull) + spread * noise[u, where, :]
                     fresh.append(value)
                     result_ref[where, :] = value
-                keep(u + 1, row, jnp.concatenate(fresh, axis=0))
+                fresh_rows.append(jnp.concatenate(fresh, axis=0))
 
             @pl.when(u < updates - 1)
             def _():
-                send_chunk(u + 1, pair)
+                for q in range(2):
+                    keep(u + 1, 2 * pair + q, fresh_rows[q])
+                if pair == rows // 2 - 2:
+                    send_early(u + 1)
 
         @pl.when(u < updates - 1)
         def _():
@@ -360,7 +382,7 @@
     lax.fori_loop(0, updates, update, 0)
 
     for u in range(updates):
-        for dt, dl, do in sent:
+        for dt, dl, do in around:
 
             @pl.when(exists(dt, dl))
             def _():
@@ -394,12 +416,11 @@
             vmem(conv_weights.shape, BF16),
             vmem(out_weight.shape, BF16),
             pltpu.SemaphoreType.DMA((7,)),
-            pltpu.SemaphoreType.DMA((updates, 27 * (rows // margin))),
-            pltpu.SemaphoreType.DMA((updates, 27 * (rows // margin))),
+            pltpu.SemaphoreType.DMA((updates, 36)),
+            pltpu.SemaphoreType.DMA((updates, 36)),
             vmem((rows, tile, cols), F32),
-            vmem((updates + 1, 3, span, 2 * tile, cols), BF16),
-            vmem((updates, 2 * tile, cols), BF16),
-            vmem((updates, 3, 3, 2, 2 * tile, cols), BF16),
+            vmem((updates, 3, span + 4, 2 * tile, cols), BF16),
+            vmem((updates, 3, 3, 2 * tile, cols), BF16),
             vmem((9 * tile, frames * LANES), F32),
             vmem((frames * hidden, 9 * tile), BF16),
             vmem((2, 2 * hidden, 12 * hidden), BF16),

time: 27.6 us -> 25.7 us (0.931)
  Pallas kernels: 26 us -> 24 us
    pallas_call x1, Pallas kernels: 26 us -> 24 us  [per_device(): pl.pallas_call(functools.partial(kernel, dims), out_shape=jax.ShapeDtypeS...]
where the time goes in v5:
time: 25.7 us; the launch traced here: 25.5 us
  Pallas kernels  24 us (93%)
  local copies, waits for them, and re-layouts  1.47 us (6%)
    pallas_call x1, Pallas kernels, per_device(): pl.pallas_call(functools.partial(kernel, dims), out_shape=jax.ShapeDtypeS...  24 us
    unnamed x1, local copies, waits for them, and re-layouts  1.47 us

profile of v5, /device:TPU:0, one launch (start us, length us, event | category | flops | bytes accessed | tf_op | source)
XLA Modules:
  0.0 25.5 jit_solution(17692962279720245485)
XLA Ops:
  0.0 24.0 %shard_map.82 = f32[128,128]{1,0:T(8,128)} custom-call(f32[2]{0:T(128)} %steps_ref.1, f32[128,128]{1,0:T(8,128)} %bitcast.8, f32[128,128]{1,0:T(8,128)} %bitcast.9, f32[128,128]{1,0:T(8,128)} %bitcast.10, f32[2,128,128]{2,1,0:T(8,128)} %bitcast.7, f32[40,96]{1,0:T(8,128)} %bitcast.11, bf16[2,9,96,96]{3,2,1,0:T(8,128)(2,1)} %conv_hbm.1, ...), custom_call_target="tpu_custom_call" | custom-call | flops 1358954496 | bytes 1048576 | tf_op jit(solution)/shard_map/pallas_call | solution.py:405
  24.0 1.5 %copy.10 = f32[2,8,8,128]{3,2,1,0:T(8,128)} copy(f32[2,8,8,128]{3,2,1,0:T(8,128)} %bitcast.6) | data formatting | bytes 131072

commit v6 on v5

--- a/solution.py
+++ b/solution.py
@@ -70,9 +70,7 @@
             )
         )
     ]
-    for load in loads:
-        load.start()
-
+    loads[0].start()
     head = margin + 1
     own_start = head + 1
     own_edge = own_start + rows
@@ -121,6 +119,9 @@
             pl.semaphore_signal(
                 barrier, inc=1, device_id=target(dt, dl, do), device_id_type=pl.DeviceIdType.MESH
             )
+
+    for load in loads[1:]:
+        load.start()
 
     def one(flag):
         return flag.astype(jnp.int32)
@@ -352,7 +353,6 @@
             )
             merged = (base.astype(F32) + second).astype(BF16)
             score = jnp.dot(out_w[...], merged, preferred_element_type=F32)
-            fresh_rows = []
             for q in range(2):
                 row = 2 * pair + q
                 fresh = []
@@ -364,13 +364,11 @@
                     value = current + step * (drift + pull) + spread * noise[u, where, :]
                     fresh.append(value)
                     result_ref[where, :] = value
-                fresh_rows.append(jnp.concatenate(fresh, axis=0))
-
-            @pl.when(u < updates - 1)
-            def _():
-                for q in range(2):
-                    keep(u + 1, 2 * pair + q, fresh_rows[q])
-                if pair == rows // 2 - 2:
+                keep(u + 1, row, jnp.concatenate(fresh, axis=0))
+            if pair == rows // 2 - 2:
+
+                @pl.when(u < updates - 1)
+                def _():
                     send_early(u + 1)
 
         @pl.when(u < updates - 1)
@@ -419,7 +417,7 @@
             pltpu.SemaphoreType.DMA((updates, 36)),
             pltpu.SemaphoreType.DMA((updates, 36)),
             vmem((rows, tile, cols), F32),
-            vmem((updates, 3, span + 4, 2 * tile, cols), BF16),
+            vmem((updates + 1, 3, span + 4, 2 * tile, cols), BF16),
             vmem((updates, 3, 3, 2 * tile, cols), BF16),
             vmem((9 * tile, frames * LANES), F32),
             vmem((frames * hidden, 9 * tile), BF16),

time: 25.7 us -> 25.2 us (0.981)
  Pallas kernels: 24 us -> 23.6 us
    pallas_call x1, Pallas kernels: 24 us -> 23.6 us  [per_device(): pl.pallas_call(functools.partial(kernel, dims), out_shape=jax.ShapeDtypeS...]
where the time goes in v6:
time: 25.2 us; the launch traced here: 25.1 us
  Pallas kernels  23.6 us (94%)
  local copies, waits for them, and re-layouts  1.47 us (6%)
    pallas_call x1, Pallas kernels, per_device(): pl.pallas_call(functools.partial(kernel, dims), out_shape=jax.ShapeDtypeS...  23.6 us
    unnamed x1, local copies, waits for them, and re-layouts  1.47 us

profile of v6, /device:TPU:0, one launch (start us, length us, event | category | flops | bytes accessed | tf_op | source)
XLA Modules:
  0.0 25.1 jit_solution(7538275433208932027)
XLA Ops:
  0.0 23.6 %shard_map.82 = f32[128,128]{1,0:T(8,128)} custom-call(f32[2]{0:T(128)} %steps_ref.1, f32[128,128]{1,0:T(8,128)} %bitcast.8, f32[128,128]{1,0:T(8,128)} %bitcast.9, f32[128,128]{1,0:T(8,128)} %bitcast.10, f32[2,128,128]{2,1,0:T(8,128)} %bitcast.7, f32[40,96]{1,0:T(8,128)} %bitcast.11, bf16[2,9,96,96]{3,2,1,0:T(8,128)(2,1)} %conv_hbm.1, ...), custom_call_target="tpu_custom_call" | custom-call | flops 1358954496 | bytes 1048576 | tf_op jit(solution)/shard_map/pallas_call | solution.py:403
  23.6 1.5 %copy.10 = f32[2,8,8,128]{3,2,1,0:T(8,128)} copy(f32[2,8,8,128]{3,2,1,0:T(8,128)} %bitcast.6) | data formatting | bytes 131072

commit v7 on v6

--- a/solution.py
+++ b/solution.py
@@ -194,13 +194,14 @@
             for dl in (-1, 1, 0):
                 send(u, dt, dl, 1)
 
-    def receive_all(u):
+    def receive(u, early):
         for dt, dl, do in around:
 
             @pl.when(exists(-dt, -dl))
             def _():
                 for chunk in chunks_of(dl, do):
-                    message(u, dt, dl, do, chunk).wait_recv()
+                    if early == (dl == 0 and not do and chunk == 0):
+                        message(u, dt, dl, do, chunk).wait_recv()
 
     def strided(frame, row):
         return pl.ds(frame * chans * rows + row, chans, stride=rows)
@@ -256,9 +257,12 @@
     low_lanes = lane_tall < cols // 2
     edge_lane = lax.broadcasted_iota(jnp.int32, (hidden, 2 * cols), 1)
 
+    def edge_lanes(row):
+        first = (group * row + group // 4 - 1) % (2 * cols)
+        return first, (group * row + 3 * group // 4) % (2 * cols)
+
     def shifted(value, edge, row, b):
-        first = (group * row + group // 4 - 1) % (2 * cols)
-        last = (group * row + 3 * group // 4) % (2 * cols)
+        first, last = edge_lanes(row)
         if b == 0:
             return jnp.concatenate([edge[:, first : first + 1], value[:, : cols - 1]], axis=1)
         if b == 2:
@@ -266,7 +270,14 @@
         return value
 
     def update(u, carry):
-        receive_all(u)
+        for dt, dl, do in around:
+
+            @pl.when(exists(dt, dl))
+            def _():
+                for chunk in chunks_of(dl, do):
+                    message(u, dt, dl, do, chunk).wait_send()
+
+        receive(u, True)
 
         def rim(slot, kind):
             same = main[u, slot, (margin, own_edge, tail)[kind]]
@@ -276,24 +287,56 @@
             row + (2 if row >= margin else 0) + (2 if row >= margin + rows else 0)
             for row in range(span)
         ]
-        blocks = [[main[u, slot, place] for slot in range(3)] for place in tiles]
-        blocks.append([rim(slot, 1).astype(BF16) for slot in range(3)])
-        blocks.append(
-            [jnp.where(low_lanes, rim(slot, 2), rim(slot, 0)).astype(BF16) for slot in range(3)]
-        )
-        stacked = jnp.concatenate(
-            [jnp.concatenate(block + [part[:tile] for part in block], axis=0) for block in blocks],
-            axis=1,
-        )
-        result = jnp.dot(lift_w[...], stacked, preferred_element_type=F32).astype(BF16)
+
+        def blocks(row):
+            return [main[u, slot, tiles[row]] for slot in range(3)]
+
+        soon = range(margin, rows)
+        late = [row for row in range(span) if row not in soon]
+
+        def lift(parts):
+            stacked = jnp.concatenate(
+                [
+                    jnp.concatenate(part + [item[:tile] for item in part], axis=0)
+                    for part in parts
+                ],
+                axis=1,
+            )
+            return jnp.dot(lift_w[...], stacked, preferred_element_type=F32).astype(BF16)
+
+        result = lift([blocks(row) for row in soon])
+        for frame in range(frames):
+            part = pl.ds(frame * cols, cols)
+            for index, row in enumerate(soon):
+                value = result[
+                    frame * hidden : (frame + 1) * hidden, index * cols : (index + 1) * cols
+                ]
+                lifted_cols[1, row, :, part] = value
+                lifted_cols[0, row, :, part] = jnp.concatenate(
+                    [value[:, cols - 1 :], value[:, : cols - 1]], axis=1
+                )
+                lifted_cols[2, row, :, part] = jnp.concatenate([value[:, 1:], value[:, :1]], axis=1)
+
+        receive(u, False)
+        ends = [rim(slot, 1).astype(BF16) for slot in range(3)]
+        far = [jnp.where(low_lanes, rim(slot, 2), rim(slot, 0)).astype(BF16) for slot in range(3)]
+        result = lift([blocks(row) for row in late] + [ends, far])
         edges = []
         for frame in range(frames):
             whole = result[frame * hidden : (frame + 1) * hidden]
             part = pl.ds(frame * cols, cols)
-            edge = whole[:, span * cols :]
+            edge = whole[:, len(late) * cols :]
             edges.append(edge)
-            for row in range(span):
-                value = whole[:, row * cols : (row + 1) * cols]
+            for row in soon:
+                first, last = edge_lanes(row - margin)
+                lifted_cols[0, row, :, part] = jnp.concatenate(
+                    [edge[:, first : first + 1], lifted_cols[0, row, :, part][:, 1:]], axis=1
+                )
+                lifted_cols[2, row, :, part] = jnp.concatenate(
+                    [lifted_cols[2, row, :, part][:, : cols - 1], edge[:, last : last + 1]], axis=1
+                )
+            for index, row in enumerate(late):
+                value = whole[:, index * cols : (index + 1) * cols]
                 for b in range(3):
                     lifted_cols[b, row, :, part] = shifted(value, edge, row - margin, b)
 
@@ -378,14 +421,6 @@
         return carry
 
     lax.fori_loop(0, updates, update, 0)
-
-    for u in range(updates):
-        for dt, dl, do in around:
-
-            @pl.when(exists(dt, dl))
-            def _():
-                for chunk in chunks_of(dl, do):
-                    message(u, dt, dl, do, chunk).wait_send()
 
 
 def per_device(

time: 25.2 us -> 24.8 us (0.984)
  Pallas kernels: 23.6 us -> 23.1 us
    pallas_call x1, Pallas kernels: 23.6 us -> 23.1 us  [per_device(): pl.pallas_call(functools.partial(kernel, dims), out_shape=jax.ShapeDtypeS...]
where the time goes in v7:
time: 24.8 us; the launch traced here: 24.6 us
  Pallas kernels  23.1 us (93%)
  local copies, waits for them, and re-layouts  1.47 us (6%)
    pallas_call x1, Pallas kernels, per_device(): pl.pallas_call(functools.partial(kernel, dims), out_shape=jax.ShapeDtypeS...  23.1 us
    unnamed x1, local copies, waits for them, and re-layouts  1.47 us

profile of v7, /device:TPU:0, one launch (start us, length us, event | category | flops | bytes accessed | tf_op | source)
XLA Modules:
  0.0 24.6 jit_solution(6425100518598679356)
XLA Ops:
  0.0 23.1 %shard_map.82 = f32[128,128]{1,0:T(8,128)} custom-call(f32[2]{0:T(128)} %steps_ref.1, f32[128,128]{1,0:T(8,128)} %bitcast.8, f32[128,128]{1,0:T(8,128)} %bitcast.9, f32[128,128]{1,0:T(8,128)} %bitcast.10, f32[2,128,128]{2,1,0:T(8,128)} %bitcast.7, f32[40,96]{1,0:T(8,128)} %bitcast.11, bf16[2,9,96,96]{3,2,1,0:T(8,128)(2,1)} %conv_hbm.1, ...), custom_call_target="tpu_custom_call" | custom-call | flops 1358954496 | bytes 1048576 | tf_op jit(solution)/shard_map/pallas_call | solution.py:438
  23.1 1.5 %copy.10 = f32[2,8,8,128]{3,2,1,0:T(8,128)} copy(f32[2,8,8,128]{3,2,1,0:T(8,128)} %bitcast.6) | data formatting | bytes 131072

commit v8 on v7

--- a/solution.py
+++ b/solution.py
@@ -261,13 +261,26 @@
         first = (group * row + group // 4 - 1) % (2 * cols)
         return first, (group * row + 3 * group // 4) % (2 * cols)
 
+    def turned_rows(row, part, value):
+        lifted_cols[1, row, :, part] = value
+        lifted_cols[0, row, :, part] = jnp.concatenate(
+            [value[:, cols - 1 :], value[:, : cols - 1]], axis=1
+        )
+        lifted_cols[2, row, :, part] = jnp.concatenate([value[:, 1:], value[:, :1]], axis=1)
+
     def shifted(value, edge, row, b):
         first, last = edge_lanes(row)
-        if b == 0:
-            return jnp.concatenate([edge[:, first : first + 1], value[:, : cols - 1]], axis=1)
-        if b == 2:
-            return jnp.concatenate([value[:, 1:], edge[:, last : last + 1]], axis=1)
-        return value
+        inner = value[:, 1 : cols - 1]
+        left = edge[:, first : first + 2] if b == 0 else edge[:, first + 1 : first + 2]
+        right = edge[:, last - 1 : last + 1] if b == 2 else edge[:, last - 1 : last]
+        parts = ([left] if b < 2 else []) + [inner] + ([right] if b > 0 else [])
+        return jnp.concatenate(parts, axis=1)
+
+    def first_conv(pair):
+        window = jnp.concatenate(
+            [lifted_cols[b, 2 * pair + r] for r in range(4) for b in range(3)], axis=0
+        )
+        return silu(jnp.dot(conv_w[0], window, preferred_element_type=F32))
 
     def update(u, carry):
         for dt, dl, do in around:
@@ -311,11 +324,12 @@
                 value = result[
                     frame * hidden : (frame + 1) * hidden, index * cols : (index + 1) * cols
                 ]
-                lifted_cols[1, row, :, part] = value
-                lifted_cols[0, row, :, part] = jnp.concatenate(
-                    [value[:, cols - 1 :], value[:, : cols - 1]], axis=1
-                )
-                lifted_cols[2, row, :, part] = jnp.concatenate([value[:, 1:], value[:, :1]], axis=1)
+                turned_rows(row, part, value)
+        ready = {
+            pair: first_conv(pair)
+            for pair in range(rows // 2 + 1)
+            if 2 * pair in soon and 2 * pair + 3 in soon
+        }
 
         receive(u, False)
         ends = [rim(slot, 1).astype(BF16) for slot in range(3)]
@@ -327,18 +341,9 @@
             part = pl.ds(frame * cols, cols)
             edge = whole[:, len(late) * cols :]
             edges.append(edge)
-            for row in soon:
-                first, last = edge_lanes(row - margin)
-                lifted_cols[0, row, :, part] = jnp.concatenate(
-                    [edge[:, first : first + 1], lifted_cols[0, row, :, part][:, 1:]], axis=1
-                )
-                lifted_cols[2, row, :, part] = jnp.concatenate(
-                    [lifted_cols[2, row, :, part][:, : cols - 1], edge[:, last : last + 1]], axis=1
-                )
             for index, row in enumerate(late):
                 value = whole[:, index * cols : (index + 1) * cols]
-                for b in range(3):
-                    lifted_cols[b, row, :, part] = shifted(value, edge, row - margin, b)
+                turned_rows(row, part, value)
 
         top = jnp.where(l == 0, 0.0, 1.0).astype(F32)
         bottom = jnp.where(l == l_size - 1, 0.0, 1.0).astype(F32)
@@ -364,10 +369,7 @@
             edges[frame] = jnp.where(after, value * bottom, value).astype(BF16)
 
         for pair in range(pairs):
-            window = jnp.concatenate(
-                [lifted_cols[b, 2 * pair + r] for r in range(4) for b in range(3)], axis=0
-            )
-            result = silu(jnp.dot(conv_w[0], window, preferred_element_type=F32))
+            result = ready[pair] if pair in ready else first_conv(pair)
             for q in range(2):
                 value = result[q * hidden : (q + 1) * hidden]
                 if pair == 0 and q == 0:

time: 24.8 us -> 24.2 us (0.976)
  Pallas kernels: 23.1 us -> 22.6 us
    pallas_call x1, Pallas kernels: 23.1 us -> 22.6 us  [per_device(): pl.pallas_call(functools.partial(kernel, dims), out_shape=jax.ShapeDtypeS...]
where the time goes in v8:
time: 24.2 us; the launch traced here: 24 us
  Pallas kernels  22.6 us (93%)
  local copies, waits for them, and re-layouts  1.47 us (6%)
    pallas_call x1, Pallas kernels, per_device(): pl.pallas_call(functools.partial(kernel, dims), out_shape=jax.ShapeDtypeS...  22.6 us
    unnamed x1, local copies, waits for them, and re-layouts  1.47 us

profile of v8, /device:TPU:0, one launch (start us, length us, event | category | flops | bytes accessed | tf_op | source)
XLA Modules:
  0.0 24.0 jit_solution(3130673680266454828)
XLA Ops:
  0.0 22.6 %shard_map.82 = f32[128,128]{1,0:T(8,128)} custom-call(f32[2]{0:T(128)} %steps_ref.1, f32[128,128]{1,0:T(8,128)} %bitcast.8, f32[128,128]{1,0:T(8,128)} %bitcast.9, f32[128,128]{1,0:T(8,128)} %bitcast.10, f32[2,128,128]{2,1,0:T(8,128)} %bitcast.7, f32[40,96]{1,0:T(8,128)} %bitcast.11, bf16[2,9,96,96]{3,2,1,0:T(8,128)(2,1)} %conv_hbm.1, ...), custom_call_target="tpu_custom_call" | custom-call | flops 1358954496 | bytes 1048576 | tf_op jit(solution)/shard_map/pallas_call | solution.py:440
  22.6 1.5 %copy.10 = f32[2,8,8,128]{3,2,1,0:T(8,128)} copy(f32[2,8,8,128]{3,2,1,0:T(8,128)} %bitcast.6) | data formatting | bytes 131072
